TPU v7x, 32 devices: a whole 2x2x4 slice. The times are simulated.
32 devices in a mesh: panel: 2 (over x), lat: 2 (over y), lon: 8 (over z, core).
Axes of the slice: x: 2, y: 2, z: 4, core: 2. Of those that a mesh axis runs over, the one named last changes fastest.
Arguments:
- fields: float32 [2, 6, 4, 256, 1024], P('panel', None, None, 'lat', 'lon'), may hold values from -6 to 6
- viscosity: float32 [2, 4, 256, 1024], P('panel', None, 'lat', 'lon'), may hold values from 0.01 to 0.1
- partner: int32 [2, 2, 64, 1], P('panel', 'lat', 'lon'), may hold values from 0 to 7; in each aligned block of 8 rows (0 to 7, 8 to 15, ..., all dimensions but the last counted through in order) at most 2 rows name the same one
- src_row: int32 [2, 2, 4096], P('panel', 'lat', 'lon'), may hold values from 0 to 126
- src_col: int32 [2, 2, 4096], P('panel', 'lat', 'lon'), may hold values from 0 to 126
- weight_id: int32 [2, 2, 4096], P('panel', 'lat', 'lon'), may hold values from 0 to 63
- border_angle: float32 [2, 2, 4096], P('panel', 'lat', 'lon'), may hold values from -3.140625 to 3.140625
- dest_cell: int32 [2, 2, 4096], P('panel', 'lat', 'lon'), may hold values from 0 to 16383, as said below
Outputs:
- new_fields: float32 [2, 6, 4, 256, 1024], P('panel', None, None, 'lat', 'lon')
- pressure: float32 [2, 4, 256, 1024], P('panel', None, 'lat', 'lon')
Inputs may be any that keep to these rules, and one draw needn't show every extreme that they name: `partner`: A border block's sources lie on the device of the other panel with the same lat index and this lon index; among the 8 blocks of one device no lon index is named by more than 2 blocks. `dest_cell`: the 512 border cells of one device are distinct cells of its block.
All inputs are finite; a program needn't handle non-finite values.
Results may differ from a plain program's by a relative error of at most 0.0002.
Values sent between devices are 32-bit elements; how exact they have to be, the bound alone decides.
A program may use at most 128 MiB of HBM per device.

v0:
```python
import math

import jax
import jax.numpy as jnp
from jax import lax
from jax.sharding import PartitionSpec as P

CAP = 2
WQ = 8


BUOYANCY = 0.5


def partner_2(block, axis, apart):
    count = lax.axis_size(axis)
    route = []
    for low in range(count):
        high = low | 1 << apart
        if high != low and high < count:
            route += [(low, high), (high, low)]
    return lax.ppermute(block, axis, route)


def padded_2(shard, sides, width):
    for axis, dim in sides:
        size, length = (lax.axis_size(axis), shard.shape[dim])
        up = [(i, (i + 1) % size) for i in range(size - 1)]
        down = [(j, i) for i, j in up]
        last = lax.slice_in_dim(shard, length - width, length, axis=dim)
        leading = lax.slice_in_dim(shard, 0, width, axis=dim)
        before = lax.ppermute(last, axis, up)
        after = lax.ppermute(leading, axis, down)
        shard = jnp.concatenate([before, shard, after], axis=dim)
    return shard


def metric(row_index, total_rows):
    colatitude = (
        math.pi / 4.0 + (row_index.astype(jnp.float32) + 0.5) * (math.pi / 2.0) / total_rows
    )
    inv_sine = 1.0 / jnp.sin(colatitude)
    return (inv_sine, inv_sine * inv_sine)


def lap_shrink(field, row_gain):
    centre = field[..., 1:-1, 1:-1]
    padded = jnp.pad(centre, [(0, 0)] * (centre.ndim - 3) + [(1, 1), (0, 0), (0, 0)])
    lat_term = field[..., 2:, 1:-1] + field[..., :-2, 1:-1] - 2.0 * centre
    lon_term = field[..., 1:-1, 2:] + field[..., 1:-1, :-2] - 2.0 * centre
    radial = padded[..., 2:, :, :] + padded[..., :-2, :, :] - 2.0 * centre
    return lat_term + row_gain[:, None] * lon_term + radial


def diverge(velocity, inv_sine):
    radial_pad = jnp.pad(velocity[0, :, 1:-1, 1:-1], ((1, 1), (0, 0), (0, 0)))
    lat_part = velocity[1, :, 2:, 1:-1] - velocity[1, :, :-2, 1:-1]
    lon_part = velocity[2, :, 1:-1, 2:] - velocity[2, :, 1:-1, :-2]
    rad_part = radial_pad[2:] - radial_pad[:-2]
    return 0.5 * (lat_part + inv_sine[:, None] * lon_part + rad_part)


def gradient(pressure, inv_sine):
    radial_pad = jnp.pad(pressure[:, 1:-1, 1:-1], ((1, 1), (0, 0), (0, 0)))
    grad_rad = 0.5 * (radial_pad[2:] - radial_pad[:-2])
    grad_lat = 0.5 * (pressure[:, 2:, 1:-1] - pressure[:, :-2, 1:-1])
    grad_lon = 0.5 * inv_sine[:, None] * (pressure[:, 1:-1, 2:] - pressure[:, 1:-1, :-2])
    return (grad_rad, grad_lat, grad_lon)


def cosine_table(length):
    mode_ids = jnp.arange(length, dtype=jnp.float32)
    cell_mid = jnp.arange(length, dtype=jnp.float32) + 0.5
    row_norm = jnp.sqrt(jnp.where(mode_ids > 0, 2.0, 1.0) / length)
    cos_table = row_norm[:, None] * jnp.cos(
        math.pi * mode_ids[:, None] * cell_mid[None, :] / length
    )
    eigenvalue = 4.0 * jnp.sin(math.pi * mode_ids / (2.0 * length)) ** 2
    return (cos_table, eigenvalue)


def coarse_divisor(levels, n_lat, n_lon):
    eig_rad = cosine_table(levels)[1]
    eig_lat = cosine_table(n_lat)[1]
    eig_lon = cosine_table(n_lon)[1]
    return (
        eig_rad[:, None, None]
        + eig_lat[None, :, None]
        + eig_lon[None, None, :]
        + 1.0 / (n_lat * n_lon)
    )


def coarse_solve(block_sum, n_lat, n_lon):
    highest = lax.Precision.HIGHEST
    tab_rad = cosine_table(block_sum.shape[0])[0]
    tab_lat = cosine_table(n_lat)[0]
    tab_lon = cosine_table(n_lon)[0]
    spectrum = jnp.einsum("kr,rlo->klo", tab_rad, block_sum, precision=highest)
    spectrum = jnp.einsum("kl,rlo->rko", tab_lat, spectrum, precision=highest)
    spectrum = jnp.einsum("ko,rlo->rlk", tab_lon, spectrum, precision=highest)
    spectrum = spectrum / coarse_divisor(block_sum.shape[0], n_lat, n_lon)
    restored = jnp.einsum("kr,klo->rlo", tab_rad, spectrum, precision=highest)
    restored = jnp.einsum("kl,rko->rlo", tab_lat, restored, precision=highest)
    restored = jnp.einsum("ko,rlk->rlo", tab_lon, restored, precision=highest)
    return restored / math.sqrt(n_lat * n_lon)


def fractions(weight_ids):
    frac_lat = ((weight_ids // WQ).astype(jnp.float32) + 0.5) / WQ
    frac_lon = ((weight_ids % WQ).astype(jnp.float32) + 0.5) / WQ
    return (frac_lat, frac_lon)


def bilinear(lower_left, lower_right, upper_left, upper_right, frac_lat, frac_lon):
    return (
        (1.0 - frac_lat) * (1.0 - frac_lon) * lower_left
        + (1.0 - frac_lat) * frac_lon * lower_right
        + frac_lat * (1.0 - frac_lon) * upper_left
        + frac_lat * frac_lon * upper_right
    )


def shards(fields, viscosity, partner, src_row, src_col, weight_id, border_angle, dest_cell):
    n_lat = lax.axis_size("lat")
    n_lon = lax.axis_size("lon")
    lat_pos = lax.axis_index("lat")
    lon_pos = lax.axis_index("lon")
    own_fields = fields[0]
    levels, rows_dev, cols_dev = (own_fields.shape[1], own_fields.shape[2], own_fields.shape[3])
    channels = 6 * levels
    blocks = partner.shape[2]
    block_cells = src_row.shape[2] // blocks
    capacity = CAP
    slot_count = n_lon * capacity
    total_rows = rows_dev * n_lat
    flat_cells = own_fields.reshape(channels, rows_dev * cols_dev)
    target = partner[0, 0, :, 0]
    onehot = (target[:, None] == jnp.arange(n_lon, dtype=jnp.int32)[None, :]).astype(jnp.int32)
    before = jnp.sum(
        (jnp.cumsum(onehot, axis=0, dtype=jnp.int32) - onehot) * onehot, axis=1, dtype=jnp.int32
    )
    slot_of = target * capacity + before
    base_cell = (src_row[0, 0] * cols_dev + src_col[0, 0]).reshape(blocks, block_cells)
    weight_ids = weight_id[0, 0].reshape(blocks, block_cells)
    empty = jnp.zeros((slot_count, block_cells), jnp.int32)
    requests = partner_2(
        empty.at[slot_of].set(base_cell).reshape(n_lon, capacity * block_cells), "panel", 0
    )
    requests = lax.all_to_all(requests, "lon", split_axis=0, concat_axis=0, tiled=True)
    served = jnp.stack(
        tuple(
            (
                jnp.take(flat_cells, requests + offset, axis=1)
                for offset in (0, 1, cols_dev, cols_dev + 1)
            )
        ),
        axis=0,
    )
    served = lax.all_to_all(served, "lon", split_axis=2, concat_axis=2, tiled=True)
    served = partner_2(served, "panel", 0)
    picked = served.reshape(4, channels, slot_count, block_cells)[:, :, slot_of, :]
    frac_lat, frac_lon = fractions(weight_ids)
    values = bilinear(picked[0], picked[1], picked[2], picked[3], frac_lat, frac_lon)
    values = values.reshape(6, levels, blocks * block_cells)
    turn = border_angle[0, 0]
    cos_angle = jnp.cos(turn)
    sin_angle = jnp.sin(turn)
    rotated = jnp.stack(
        [
            values[0],
            cos_angle * values[1] + sin_angle * values[2],
            cos_angle * values[2] - sin_angle * values[1],
            values[3],
            cos_angle * values[4] + sin_angle * values[5],
            cos_angle * values[5] - sin_angle * values[4],
        ],
        axis=0,
    ).reshape(channels, blocks * block_cells)
    filled = flat_cells.at[:, dest_cell[0, 0]].set(rotated).reshape(6, levels, rows_dev, cols_dev)
    diffusivity = viscosity[0]
    inv_own, gain_own = metric(
        lat_pos * rows_dev + jnp.arange(-0, rows_dev + 0, dtype=jnp.int32), total_rows
    )
    widened = padded_2(filled, (("lat", 2), ("lon", 3)), 1)
    stepped = filled + diffusivity[None] * lap_shrink(widened, gain_own)
    stepped = jnp.concatenate([stepped[0:1] + BUOYANCY * filled[3:4], stepped[1:]], axis=0)
    velocity = padded_2(stepped[0:3], (("lat", 2), ("lon", 3)), 1)
    divergence = diverge(velocity, inv_own)
    press_one = -divergence / (4.0 + 2.0 * gain_own)[:, None]
    press_wide = padded_2(press_one, (("lat", 1), ("lon", 2)), 1)
    resid_one = -divergence + lap_shrink(press_wide, gain_own)
    block_sum = jnp.sum(resid_one, axis=(1, 2)) * (1.0 / math.sqrt(rows_dev * cols_dev))
    gathered = lax.all_gather(block_sum[:, None], ("lat", "lon"), axis=1, tiled=True)
    coarse = coarse_solve(gathered.reshape(levels, n_lat, n_lon), n_lat, n_lon)
    start = jnp.zeros((), jnp.int32)
    own_coarse = lax.dynamic_slice(coarse, (start, lat_pos, lon_pos), (levels, 1, 1)).reshape(
        levels
    )
    pressure = press_one + own_coarse[:, None, None]
    press_rim = padded_2(pressure, (("lat", 1), ("lon", 2)), 1)
    grad_rad, grad_lat, grad_lon = gradient(press_rim, inv_own)
    result = jnp.stack(
        [
            stepped[0] - grad_rad,
            stepped[1] - grad_lat,
            stepped[2] - grad_lon,
            stepped[3],
            stepped[4],
            stepped[5],
        ],
        axis=0,
    )
    return (result[None], pressure[None])


def solution(mesh):
    return jax.shard_map(
        shards,
        mesh=mesh,
        in_specs=(
            P("panel", None, None, "lat", "lon"),
            P("panel", None, "lat", "lon"),
            P("panel", "lat", "lon", None),
            P("panel", "lat", "lon"),
            P("panel", "lat", "lon"),
            P("panel", "lat", "lon"),
            P("panel", "lat", "lon"),
            P("panel", "lat", "lon"),
        ),
        out_specs=(P("panel", None, None, "lat", "lon"), P("panel", None, "lat", "lon")),
        check_vma=False,
    )
```

profile of v0, /device:TPU:0, one launch (start us, length us, event | category | flops | bytes accessed | tf_op | source)
XLA Modules:
  0.0 206.3 jit_solution(5277321169143282194)
XLA Ops:
  4.4 2.9 %collective-permute-start = (s32[8,128]{1,0:T(8,128)S(1)}, s32[8,128]{1,0:T(8,128)}, u32[]{:S(2)}, u32[]{:S(2)}) collective-permute-start(s32[8,128]{1,0:T(8,128)S(1)} %reshape.637), channel_id=1, source_target_pairs={{0,16},{16,0},{1,17},{17,1},{2,18},{18,2},{3,19},{19,3},{4,20},{20... | collective-permute-start | bytes 12296 | tf_op jit(solution)/shard_map/ppermute | solution.py:22
  7.4 1.6 collective-permute-done
  9.0 5.4 %all-to-all-start = ((s32[8,1,128]{2,1,0:T(1,128)}), s32[8,1,128]{2,1,0:T(1,128)S(1)}, u32[]{:S(2)}, u32[]{:S(2)}) async-start(s32[8,1,128]{2,1,0:T(1,128)} %bitcast.6), calls=%async_computation | async-start | bytes 8192 | tf_op jit(solution)/shard_map/all_to_all | solution.py:150
  14.5 2.3 %copy.186 = f32[3,8,128,128]{3,1,2,0:T(8,128)S(1)} copy(f32[3,8,128,128]{3,2,1,0:T(8,128)} %bitcast.163) | data formatting | bytes 3145728
  16.8 4.7 %copy.143 = f32[24,16384]{0,1:T(8,128)} copy(f32[24,16384]{1,0:T(8,128)S(1)} %bitcast.161) | data formatting | bytes 3145728 | tf_op jit(solution)/shard_map/reshape;squeeze | solution.py:137
  21.5 6.2 %gather_fusion.1 = f32[1024,24]{1,0:T(8,128)S(1)} fusion(f32[24,16384]{0,1:T(8,128)} %copy.143, s32[1024]{0:T(1024)S(1)} %get-tuple-element.38), kind=kCustom, calls=%fused_computation.clone | custom fusion | bytes 200704 | tf_op jit(solution)/shard_map/jit(_take)/gather | solution.py:154
  27.9 6.2 %gather_fusion.2 = f32[1024,24]{1,0:T(8,128)S(1)} fusion(f32[24,16384]{0,1:T(8,128)} %copy.143, s32[1024]{0:T(1024)S(1)} %get-tuple-element.39), kind=kCustom, calls=%fused_computation.1.clone | custom fusion | bytes 200704 | tf_op jit(solution)/shard_map/jit(_take)/gather | solution.py:154
  34.2 6.2 %gather_fusion.3 = f32[1024,24]{1,0:T(8,128)S(1)} fusion(f32[24,16384]{0,1:T(8,128)} %copy.143, s32[1024]{0:T(1024)S(1)} %get-tuple-element.40), kind=kCustom, calls=%fused_computation.2.clone | custom fusion | bytes 200704 | tf_op jit(solution)/shard_map/jit(_take)/gather | solution.py:154
  40.6 6.2 %gather_fusion.4 = f32[1024,24]{1,0:T(8,128)S(1)} fusion(f32[24,16384]{0,1:T(8,128)} %copy.143, s32[1024]{0:T(1024)S(1)} %get-tuple-element.41), kind=kCustom, calls=%fused_computation.3.clone | custom fusion | bytes 200704 | tf_op jit(solution)/shard_map/jit(_take)/gather | solution.py:154
  47.9 5.1 %all-to-all-start.1 = ((f32[4,24,8,128]{3,1,0,2:T(8,128)}), f32[4,24,8,128]{3,1,0,2:T(8,128)S(1)}, u32[]{:S(2)}, u32[]{:S(2)}) async-start(f32[4,24,8,128]{3,1,0,2:T(8,128)} %pad_maximum_fusion.10), calls=%async_computation.1 | async-start | bytes 786432 | tf_op jit(solution)/shard_map/all_to_all | solution.py:160
  54.4 11.1 %all-to-all-done.1 = f32[4,24,8,128]{3,1,0,2:T(8,128)S(1)} async-done(((f32[4,24,8,128]{3,1,0,2:T(8,128)}), f32[4,24,8,128]{3,1,0,2:T(8,128)S(1)}, u32[]{:S(2)}, u32[]{:S(2)}) %all-to-all-start.1) | async-done | bytes 393248 | tf_op jit(solution)/shard_map/all_to_all | solution.py:160
  65.5 1.5 collective-permute-start.1
  67.1 9.1 %collective-permute-done.1 = f32[4,24,8,128]{3,1,0,2:T(8,128)S(1)} collective-permute-done((f32[4,24,8,128]{3,1,0,2:T(8,128)S(1)}, f32[4,24,8,128]{3,1,0,2:T(8,128)S(1)}, u32[]{:S(2)}, u32[]{:S(2)}) %collective-permute-start.1) | collective-permute-done | bytes 393248 | tf_op jit(solution)/shard_map/ppermute | solution.py:22
  78.2 8.3 %scatter_fusion = f32[24,16384]{0,1:T(8,128)} fusion(f32[24,16384]{0,1:T(8,128)} %copy.143, s32[512]{0:T(512)S(1)} %bitcast.181, f32[512,24]{1,0:T(8,128)S(1)} %copy.144), kind=kCustom, calls=%fused_computation.6 | custom fusion | bytes 149504 | tf_op jit(solution)/shard_map/scatter | solution.py:180
  86.6 5.1 %copy.145 = f32[24,16384]{1,0:T(8,128)S(1)} copy(f32[24,16384]{0,1:T(8,128)} %scatter_fusion) | data formatting | bytes 3145728 | tf_op jit(solution)/shard_map/scatter | solution.py:180
  92.0 1.3 collective-permute-start.2
  93.3 4.5 %collective-permute-start.3 = (f32[6,4,1,128]{3,2,1,0:T(1,128)S(1)}, f32[6,4,1,128]{3,2,1,0:T(1,128)S(1)}, u32[]{:S(2)}, u32[]{:S(2)}) collective-permute-start(f32[6,4,1,128]{3,2,1,0:T(1,128)S(1)} %get-tuple-element.11), channel_id=1, source_target_pairs={{0,8},{1,9},{2,10},{3,11},{4,12},{5,13},{6,14},{7,15},{16,24},{17,... | collective-permute-start | bytes 36872 | tf_op jit(solution)/shard_map/ppermute | solution.py:32
  97.9 1.3 collective-permute-done.3
  99.4 2.3 %fusion.118 = (f32[6,4,130,1]{3,2,1,0:T(8,128)}, f32[6,4,130,1]{3,2,1,0:T(8,128)}) fusion(f32[6,4,130,128]{3,2,1,0:T(8,128)S(1)} %pad_maximum_fusion), kind=kLoop, calls=%fused_computation.249 | loop fusion | bytes 49920 | tf_op jit(solution)/shard_map/slice | solution.py:31
  101.7 2.3 %copy.146 = f32[6,4,130,1]{2,1,3,0:T(4,128)S(1)} copy(f32[6,4,130,1]{3,2,1,0:T(8,128)} %get-tuple-element.7) | data formatting | bytes 24960 | tf_op jit(solution)/shard_map/slice | solution.py:31
  104.0 1.3 collective-permute-start.4
  105.3 2.3 %copy.148 = f32[6,4,130,1]{2,1,3,0:T(4,128)S(1)} copy(f32[6,4,130,1]{3,2,1,0:T(8,128)} %get-tuple-element.8) | data formatting | bytes 24960 | tf_op jit(solution)/shard_map/slice | solution.py:30
  107.6 3.0 %collective-permute-start.5 = (f32[6,4,130,1]{2,1,3,0:T(4,128)S(1)}, f32[6,4,130,1]{2,1,3,0:T(4,128)S(1)}, u32[]{:S(2)}, u32[]{:S(2)}) collective-permute-start(f32[6,4,130,1]{2,1,3,0:T(4,128)S(1)} %copy.148), channel_id=1, source_target_pairs={{0,1},{1,2},{2,3},{3,4},{4,5},{5,6},{6,7},{8,9},{9,10},{10,11},{11... | collective-permute-start | bytes 37448 | tf_op jit(solution)/shard_map/ppermute | solution.py:32
  110.7 6.6 %slice_multiply_fusion = f32[4,16384]{0,1:T(8,128)} fusion(f32[24,16384]{0,1:T(8,128)} %scatter_fusion), kind=kLoop, calls=%fused_computation.7 | loop fusion | flops 65536 | bytes 524288 | tf_op jit(solution)/shard_map/mul | solution.py:187
  117.3 5.2 %copy.150 = f32[1,4,128,128]{3,2,1,0:T(8,128)S(1)} copy(f32[1,4,128,128]{1,3,2,0:T(8,128)} %bitcast.156) | data formatting | bytes 524288 | tf_op jit(solution)/shard_map/mul | solution.py:187
  122.5 1.8 copy.147
  124.3 1.8 copy.149
  126.1 3.5 %fusion.4 = f32[6,4,128,128]{3,2,1,0:T(8,128)S(1)} fusion(f32[6,4,128,128]{3,2,1,0:T(8,128)S(1)} %bitcast.159, f32[6,4,130,1]{3,2,1,0:T(8,128)} %copy.149, f32[6,4,1,128]{3,2,1,0:T(1,128)S(1)} %collective-permute-done.2, f32[6,4,1,128]{3,2,1,0:T(1,128)S(1)} %collective-permute-done.3, f32[6,4,130,1]{3,2,1,0:T(8,128)} %copy.147, f32[128]{0:T(128)S(1)} %fusion.115, ...), kind=kLoop, calls=%fused_computation.19 | loop fusion | flops 7864320 | bytes 3457920 | tf_op jit(solution)/shard_map/add | solution.py:186
  129.7 1.3 collective-permute-start.6
  131.0 4.7 %collective-permute-start.7 = (f32[3,4,1,128]{3,2,1,0:T(1,128)S(1)}, f32[3,4,1,128]{3,2,1,0:T(1,128)S(1)}, u32[]{:S(2)}, u32[]{:S(2)}) collective-permute-start(f32[3,4,1,128]{3,2,1,0:T(1,128)S(1)} %get-tuple-element.9), channel_id=1, source_target_pairs={{0,8},{1,9},{2,10},{3,11},{4,12},{5,13},{6,14},{7,15},{16,24},{17,... | collective-permute-start | bytes 18440 | tf_op jit(solution)/shard_map/ppermute | solution.py:32
  137.0 1.4 fusion.120
  138.4 1.6 copy.151
  140.1 1.3 collective-permute-start.8
  141.4 1.6 copy.153
  143.0 3.0 %collective-permute-start.9 = (f32[3,4,130,1]{2,1,3,0:T(4,128)S(1)}, f32[3,4,130,1]{2,1,3,0:T(4,128)S(1)}, u32[]{:S(2)}, u32[]{:S(2)}) collective-permute-start(f32[3,4,130,1]{2,1,3,0:T(4,128)S(1)} %copy.153), channel_id=1, source_target_pairs={{0,1},{1,2},{2,3},{3,4},{4,5},{5,6},{6,7},{8,9},{9,10},{10,11},{11... | collective-permute-start | bytes 18728 | tf_op jit(solution)/shard_map/ppermute | solution.py:32
  146.0 1.3 copy.152
  148.5 1.4 broadcast_divide_fusion
  149.9 1.3 collective-permute-start.10
  151.2 4.5 %collective-permute-start.11 = (f32[4,1,128]{2,1,0:T(1,128)S(1)}, f32[4,1,128]{2,1,0:T(1,128)S(1)}, u32[]{:S(2)}, u32[]{:S(2)}) collective-permute-start(f32[4,1,128]{2,1,0:T(1,128)S(1)} %get-tuple-element.22), channel_id=1, source_target_pairs={{0,8},{1,9},{2,10},{3,11},{4,12},{5,13},{6,14},{7,15},{16,24},{17,... | collective-permute-start | bytes 6152 | tf_op jit(solution)/shard_map/ppermute | solution.py:32
  155.8 1.3 collective-permute-done.11
  157.9 1.3 collective-permute-start.12
  159.2 3.0 %collective-permute-start.13 = (f32[4,130,1]{2,1,0:T(8,128)S(1)}, f32[4,130,1]{2,1,0:T(8,128)S(1)}, u32[]{:S(2)}, u32[]{:S(2)}) collective-permute-start(f32[4,130,1]{2,1,0:T(8,128)S(1)} %get-tuple-element.18), channel_id=1, source_target_pairs={{0,1},{1,2},{2,3},{3,4},{4,5},{5,6},{6,7},{8,9},{9,10},{10,11},{11... | collective-permute-start | bytes 6248 | tf_op jit(solution)/shard_map/ppermute | solution.py:32
  163.8 26.1 %all-gather = f32[16,1,4]{2,1,0:T(1,128)S(1)} all-gather(f32[1,1,4]{2,1,0:T(1,128)S(1)} %multiply_bitcast_fusion), channel_id=1, replica_groups=mesh['panel'=2,'lat'=2,'lon'=8] {'lat','lon'}, dimensions={0}, use_global_device_ids=true | all-gather | bytes 272 | tf_op jit(solution)/shard_map/all_gather | solution.py:194
  191.9 1.3 collective-permute-start.14
  193.2 4.5 %collective-permute-start.15 = (f32[4,1,128]{2,1,0:T(1,128)S(1)}, f32[4,1,128]{2,1,0:T(1,128)S(1)}, u32[]{:S(2)}, u32[]{:S(2)}) collective-permute-start(f32[4,1,128]{2,1,0:T(1,128)S(1)} %get-tuple-element.20), channel_id=1, source_target_pairs={{0,8},{1,9},{2,10},{3,11},{4,12},{5,13},{6,14},{7,15},{16,24},{17,... | collective-permute-start | bytes 6152 | tf_op jit(solution)/shard_map/ppermute | solution.py:32
  199.2 1.3 collective-permute-start.16
  200.5 3.0 %collective-permute-start.17 = (f32[4,130,1]{2,1,0:T(8,128)S(1)}, f32[4,130,1]{2,1,0:T(8,128)S(1)}, u32[]{:S(2)}, u32[]{:S(2)}) collective-permute-start(f32[4,130,1]{2,1,0:T(8,128)S(1)} %get-tuple-element.16), channel_id=1, source_target_pairs={{0,1},{1,2},{2,3},{3,4},{4,5},{5,6},{6,7},{8,9},{9,10},{10,11},{11... | collective-permute-start | bytes 6248 | tf_op jit(solution)/shard_map/ppermute | solution.py:32
  205.0 1.3 maximum_bitcast_fusion
  (113 shorter events, 19.3 us)
Async XLA Ops:
  4.4 4.6 %collective-permute-start = (s32[8,128]{1,0:T(8,128)S(1)}, s32[8,128]{1,0:T(8,128)}, u32[]{:S(2)}, u32[]{:S(2)}) collective-permute-start(s32[8,128]{1,0:T(8,128)S(1)} %reshape.637), channel_id=1, source_target_pairs={{0,16},{16,0},{1,17},{17,1},{2,18},{18,2},{3,19},{19,3},{4,20},{20... | collective-permute-start | bytes 12296 | tf_op jit(solution)/shard_map/ppermute | solution.py:22
  9.0 12.5 %all-to-all-start = ((s32[8,1,128]{2,1,0:T(1,128)}), s32[8,1,128]{2,1,0:T(1,128)S(1)}, u32[]{:S(2)}, u32[]{:S(2)}) async-start(s32[8,1,128]{2,1,0:T(1,128)} %bitcast.6), calls=%async_computation | async-start | bytes 8192 | tf_op jit(solution)/shard_map/all_to_all | solution.py:150
  46.8 6.7 %copy-start.1 = (s32[1,1,512]{2,1,0:T(1,128)S(1)}, s32[1,1,512]{2,1,0:T(1,128)}, u32[]{:S(2)}) copy-start(s32[1,1,512]{2,1,0:T(1,128)} %param.15) | copy-start | bytes 6148
  46.8 7.5 %copy-start.2 = (s32[1,1,512]{2,1,0:T(1,128)S(1)}, s32[1,1,512]{2,1,0:T(1,128)}, u32[]{:S(2)}) copy-start(s32[1,1,512]{2,1,0:T(1,128)} %param.17) | copy-start | bytes 6148
  46.8 7.5 %copy-start = (f32[1,1,512]{2,1,0:T(1,128)S(1)}, f32[1,1,512]{2,1,0:T(1,128)}, u32[]{:S(2)}) copy-start(f32[1,1,512]{2,1,0:T(1,128)} %param.16) | copy-start | bytes 6148
  47.9 17.7 %all-to-all-start.1 = ((f32[4,24,8,128]{3,1,0,2:T(8,128)}), f32[4,24,8,128]{3,1,0,2:T(8,128)S(1)}, u32[]{:S(2)}, u32[]{:S(2)}) async-start(f32[4,24,8,128]{3,1,0,2:T(8,128)} %pad_maximum_fusion.10), calls=%async_computation.1 | async-start | bytes 786432 | tf_op jit(solution)/shard_map/all_to_all | solution.py:160
  65.5 10.7 %collective-permute-start.1 = (f32[4,24,8,128]{3,1,0,2:T(8,128)S(1)}, f32[4,24,8,128]{3,1,0,2:T(8,128)S(1)}, u32[]{:S(2)}, u32[]{:S(2)}) collective-permute-start(f32[4,24,8,128]{3,1,0,2:T(8,128)S(1)} %all-to-all-done.1), channel_id=1, source_target_pairs={{0,16},{16,0},{1,17},{17,1},{2,18},{18,2},{3,19},{19,3},{4,20},{20... | collective-permute-start | bytes 1179656 | tf_op jit(solution)/shard_map/ppermute | solution.py:22
  92.0 5.9 %collective-permute-start.2 = (f32[6,4,1,128]{3,2,1,0:T(1,128)S(1)}, f32[6,4,1,128]{3,2,1,0:T(1,128)S(1)}, u32[]{:S(2)}, u32[]{:S(2)}) collective-permute-start(f32[6,4,1,128]{3,2,1,0:T(1,128)S(1)} %get-tuple-element.12), channel_id=1, source_target_pairs={{8,0},{9,1},{10,2},{11,3},{12,4},{13,5},{14,6},{15,7},{24,16},{25,... | collective-permute-start | bytes 36872 | tf_op jit(solution)/shard_map/ppermute | solution.py:33
  93.3 5.9 %collective-permute-start.3 = (f32[6,4,1,128]{3,2,1,0:T(1,128)S(1)}, f32[6,4,1,128]{3,2,1,0:T(1,128)S(1)}, u32[]{:S(2)}, u32[]{:S(2)}) collective-permute-start(f32[6,4,1,128]{3,2,1,0:T(1,128)S(1)} %get-tuple-element.11), channel_id=1, source_target_pairs={{0,8},{1,9},{2,10},{3,11},{4,12},{5,13},{6,14},{7,15},{16,24},{17,... | collective-permute-start | bytes 36872 | tf_op jit(solution)/shard_map/ppermute | solution.py:32
  104.0 18.5 %collective-permute-start.4 = (f32[6,4,130,1]{2,1,3,0:T(4,128)S(1)}, f32[6,4,130,1]{2,1,3,0:T(4,128)S(1)}, u32[]{:S(2)}, u32[]{:S(2)}) collective-permute-start(f32[6,4,130,1]{2,1,3,0:T(4,128)S(1)} %copy.146), channel_id=1, source_target_pairs={{1,0},{2,1},{3,2},{4,3},{5,4},{6,5},{7,6},{9,8},{10,9},{11,10},{12... | collective-permute-start | bytes 37448 | tf_op jit(solution)/shard_map/ppermute | solution.py:33
  107.6 16.6 %collective-permute-start.5 = (f32[6,4,130,1]{2,1,3,0:T(4,128)S(1)}, f32[6,4,130,1]{2,1,3,0:T(4,128)S(1)}, u32[]{:S(2)}, u32[]{:S(2)}) collective-permute-start(f32[6,4,130,1]{2,1,3,0:T(4,128)S(1)} %copy.148), channel_id=1, source_target_pairs={{0,1},{1,2},{2,3},{3,4},{4,5},{5,6},{6,7},{8,9},{9,10},{10,11},{11... | collective-permute-start | bytes 37448 | tf_op jit(solution)/shard_map/ppermute | solution.py:32
  129.7 6.1 %collective-permute-start.6 = (f32[3,4,1,128]{3,2,1,0:T(1,128)S(1)}, f32[3,4,1,128]{3,2,1,0:T(1,128)S(1)}, u32[]{:S(2)}, u32[]{:S(2)}) collective-permute-start(f32[3,4,1,128]{3,2,1,0:T(1,128)S(1)} %get-tuple-element.10), channel_id=1, source_target_pairs={{8,0},{9,1},{10,2},{11,3},{12,4},{13,5},{14,6},{15,7},{24,16},{25,... | collective-permute-start | bytes 18440 | tf_op jit(solution)/shard_map/ppermute | solution.py:33
  131.0 5.9 %collective-permute-start.7 = (f32[3,4,1,128]{3,2,1,0:T(1,128)S(1)}, f32[3,4,1,128]{3,2,1,0:T(1,128)S(1)}, u32[]{:S(2)}, u32[]{:S(2)}) collective-permute-start(f32[3,4,1,128]{3,2,1,0:T(1,128)S(1)} %get-tuple-element.9), channel_id=1, source_target_pairs={{0,8},{1,9},{2,10},{3,11},{4,12},{5,13},{6,14},{7,15},{16,24},{17,... | collective-permute-start | bytes 18440 | tf_op jit(solution)/shard_map/ppermute | solution.py:32
  140.1 6.0 %collective-permute-start.8 = (f32[3,4,130,1]{2,1,3,0:T(4,128)S(1)}, f32[3,4,130,1]{2,1,3,0:T(4,128)S(1)}, u32[]{:S(2)}, u32[]{:S(2)}) collective-permute-start(f32[3,4,130,1]{2,1,3,0:T(4,128)S(1)} %copy.151), channel_id=1, source_target_pairs={{1,0},{2,1},{3,2},{4,3},{5,4},{6,5},{7,6},{9,8},{10,9},{11,10},{12... | collective-permute-start | bytes 18728 | tf_op jit(solution)/shard_map/ppermute | solution.py:33
  143.0 4.3 %collective-permute-start.9 = (f32[3,4,130,1]{2,1,3,0:T(4,128)S(1)}, f32[3,4,130,1]{2,1,3,0:T(4,128)S(1)}, u32[]{:S(2)}, u32[]{:S(2)}) collective-permute-start(f32[3,4,130,1]{2,1,3,0:T(4,128)S(1)} %copy.153), channel_id=1, source_target_pairs={{0,1},{1,2},{2,3},{3,4},{4,5},{5,6},{6,7},{8,9},{9,10},{10,11},{11... | collective-permute-start | bytes 18728 | tf_op jit(solution)/shard_map/ppermute | solution.py:32
  149.9 5.9 %collective-permute-start.10 = (f32[4,1,128]{2,1,0:T(1,128)S(1)}, f32[4,1,128]{2,1,0:T(1,128)S(1)}, u32[]{:S(2)}, u32[]{:S(2)}) collective-permute-start(f32[4,1,128]{2,1,0:T(1,128)S(1)} %get-tuple-element.23), channel_id=1, source_target_pairs={{8,0},{9,1},{10,2},{11,3},{12,4},{13,5},{14,6},{15,7},{24,16},{25,... | collective-permute-start | bytes 6152 | tf_op jit(solution)/shard_map/ppermute | solution.py:33
  151.2 5.8 %collective-permute-start.11 = (f32[4,1,128]{2,1,0:T(1,128)S(1)}, f32[4,1,128]{2,1,0:T(1,128)S(1)}, u32[]{:S(2)}, u32[]{:S(2)}) collective-permute-start(f32[4,1,128]{2,1,0:T(1,128)S(1)} %get-tuple-element.22), channel_id=1, source_target_pairs={{0,8},{1,9},{2,10},{3,11},{4,12},{5,13},{6,14},{7,15},{16,24},{17,... | collective-permute-start | bytes 6152 | tf_op jit(solution)/shard_map/ppermute | solution.py:32
  157.9 4.4 %collective-permute-start.12 = (f32[4,130,1]{2,1,0:T(8,128)}, f32[4,130,1]{2,1,0:T(8,128)S(1)}, u32[]{:S(2)}, u32[]{:S(2)}) collective-permute-start(f32[4,130,1]{2,1,0:T(8,128)} %get-tuple-element.17), channel_id=1, source_target_pairs={{1,0},{2,1},{3,2},{4,3},{5,4},{6,5},{7,6},{9,8},{10,9},{11,10},{12... | collective-permute-start | bytes 6248 | tf_op jit(solution)/shard_map/ppermute | solution.py:33
  159.2 4.2 %collective-permute-start.13 = (f32[4,130,1]{2,1,0:T(8,128)S(1)}, f32[4,130,1]{2,1,0:T(8,128)S(1)}, u32[]{:S(2)}, u32[]{:S(2)}) collective-permute-start(f32[4,130,1]{2,1,0:T(8,128)S(1)} %get-tuple-element.18), channel_id=1, source_target_pairs={{0,1},{1,2},{2,3},{3,4},{4,5},{5,6},{6,7},{8,9},{9,10},{10,11},{11... | collective-permute-start | bytes 6248 | tf_op jit(solution)/shard_map/ppermute | solution.py:32
  191.9 6.0 %collective-permute-start.14 = (f32[4,1,128]{2,1,0:T(1,128)S(1)}, f32[4,1,128]{2,1,0:T(1,128)S(1)}, u32[]{:S(2)}, u32[]{:S(2)}) collective-permute-start(f32[4,1,128]{2,1,0:T(1,128)S(1)} %get-tuple-element.21), channel_id=1, source_target_pairs={{8,0},{9,1},{10,2},{11,3},{12,4},{13,5},{14,6},{15,7},{24,16},{25,... | collective-permute-start | bytes 6152 | tf_op jit(solution)/shard_map/ppermute | solution.py:33
  193.2 5.8 %collective-permute-start.15 = (f32[4,1,128]{2,1,0:T(1,128)S(1)}, f32[4,1,128]{2,1,0:T(1,128)S(1)}, u32[]{:S(2)}, u32[]{:S(2)}) collective-permute-start(f32[4,1,128]{2,1,0:T(1,128)S(1)} %get-tuple-element.20), channel_id=1, source_target_pairs={{0,8},{1,9},{2,10},{3,11},{4,12},{5,13},{6,14},{7,15},{16,24},{17,... | collective-permute-start | bytes 6152 | tf_op jit(solution)/shard_map/ppermute | solution.py:32
  199.2 5.1 %collective-permute-start.16 = (f32[4,130,1]{2,1,0:T(8,128)S(1)}, f32[4,130,1]{2,1,0:T(8,128)S(1)}, u32[]{:S(2)}, u32[]{:S(2)}) collective-permute-start(f32[4,130,1]{2,1,0:T(8,128)S(1)} %get-tuple-element.15), channel_id=1, source_target_pairs={{1,0},{2,1},{3,2},{4,3},{5,4},{6,5},{7,6},{9,8},{10,9},{11,10},{12... | collective-permute-start | bytes 6248 | tf_op jit(solution)/shard_map/ppermute | solution.py:33
  200.5 4.2 %collective-permute-start.17 = (f32[4,130,1]{2,1,0:T(8,128)S(1)}, f32[4,130,1]{2,1,0:T(8,128)S(1)}, u32[]{:S(2)}, u32[]{:S(2)}) collective-permute-start(f32[4,130,1]{2,1,0:T(8,128)S(1)} %get-tuple-element.16), channel_id=1, source_target_pairs={{0,1},{1,2},{2,3},{3,4},{4,5},{5,6},{6,7},{8,9},{9,10},{10,11},{11... | collective-permute-start | bytes 6248 | tf_op jit(solution)/shard_map/ppermute | solution.py:32
where the time goes:
time: 210 us; the launch traced here: 206 us
  local copies, waits for them, and re-layouts  73.7 us (35%)
  starting transfers between devices  55.8 us (27%)
  waiting for transfers between devices  28.1 us (13%)
  blocking collectives  26.1 us (12%)
  other arithmetic  19.7 us (9%)
    ppermute x8, starting transfers between devices, padded_2(): before = lax.ppermute(last, axis, up)  30.5 us
    all_gather x1, blocking collectives, shards(): lax.all_gather(block_sum[:, None], ('lat', 'lon'), axis=1, tiled=True)  26.1 us
    gather x8, local copies, waits for them, and re-layouts, shards(): jnp.take(flat_cells, requests + offset, axis=1)  25.4 us
    scatter x2, local copies, waits for them, and re-layouts, shards(): flat_cells.at[:, dest_cell[0, 0]].set(rotated)  13.4 us
    all_to_all x1, waiting for transfers between devices, shards(): lax.all_to_all(served, 'lon', split_axis=2, concat_axis=2, tiled=True)  11.1 us
    ppermute x2, waiting for transfers between devices, partner_2(): return lax.ppermute(block, axis, route)  10.7 us
    ppermute x8, starting transfers between devices, padded_2(): after = lax.ppermute(leading, axis, down)  10.3 us
    slice x6, local copies, waits for them, and re-layouts, padded_2(): leading = lax.slice_in_dim(shard, 0, width, axis=dim)  8.6 us
  transfers between devices with their start and end apart: 20, of which 9 were waited for; matrix products, arithmetic and copies ran while one was open for 14% of the time, Pallas kernels for 0%

commit v1 on v0

v1 whole, which is shorter than its diff:
```python
import functools
import math

import jax
import jax.numpy as jnp
import numpy as np
from jax import lax
from jax.experimental import pallas as pl
from jax.experimental.pallas import tpu as pltpu
from jax.sharding import PartitionSpec as P

MESH = pl.DeviceIdType.MESH
WQ = 8
BUOYANCY = 0.5
TOP = 8
F32 = jnp.float32
BF16 = jnp.bfloat16


def coarse_operator(levels, n_lat, n_lon):
    def table(n):
        m = np.arange(n, dtype=np.float64)
        norm = np.sqrt(np.where(m > 0, 2.0, 1.0) / n)
        q = norm[:, None] * np.cos(np.pi * m[:, None] * (m[None, :] + 0.5) / n)
        return q, 4.0 * np.sin(np.pi * m / (2.0 * n)) ** 2

    qr, er = table(levels)
    qa, ea = table(n_lat)
    qo, eo = table(n_lon)
    inv = 1.0 / (
        ea[:, None, None] + eo[None, :, None] + er[None, None, :] + 1.0 / (n_lat * n_lon)
    )
    q = np.einsum("ax,oy,rz->aorxyz", qa, qo, qr).reshape(inv.size, inv.size)
    full = (q.T * inv.reshape(-1)) @ q / math.sqrt(n_lat * n_lon)
    count = inv.size
    wide = np.zeros((count, 8 * 128), np.float32)
    wide[:, :count] = full
    return wide.reshape(n_lat * n_lon, levels, 8, 128)


def windows(levels):
    spans, at = [], 0
    for width in (3, 3, 3, 2, 1, 1):
        for _ in range(levels):
            spans.append((at + width, width))
            at += 2 * width
    return spans


def visc_windows(levels):
    return [(4 * k + 2, 2) for k in range(levels)]


def pack(tiles, spans, lane):
    packed = None
    for tile, (centre, width) in zip(tiles, spans):
        moved = pltpu.roll(tile, centre, 1)
        inside = (lane >= centre - width) & (lane < centre + width)
        packed = jnp.where(inside, moved, 0.0 if packed is None else packed)
    return packed


def right_part(spans, lane):
    mask = jnp.zeros(lane.shape, jnp.int32)
    for centre, width in spans:
        mask = jnp.where((lane >= centre) & (lane < centre + width), 1, mask)
    return mask > 0


def unpack(merged, span, lane):
    centre, width = span
    moved = pltpu.roll(merged, (128 - centre) % 128, 1)
    return jnp.where((lane < width) | (lane >= 128 - width), moved, 0.0)


def kernel(
    dims,
    partner_ref, row_ref, col_ref, wid_ref, ang_ref, dest_ref, fields_ref, visc_ref, oper_ref,
    out_ref, press_ref,
    fld, fcat, ask, asked, reply, answer, x, hx, pk, pkl, pkr, va, vh, vpk, vpl, vpr,
    inv_s, gain_s, coef_a, coef_h, st, sth, p1, p1h, hit_s, rmask, cmask,
    opr, sums, mine, onew, opress,
    in_sem, op_sem, out_sem, ask_send, ask_recv, rep_send, rep_recv,
    halo_send, halo_recv, v_send, v_recv, sum_send, sum_recv,
):
    n_lat, n_lon, levels, blocks = dims
    ndev = n_lat * n_lon
    channels = 6 * levels
    rows_ext = 128 + 2 * TOP
    pairs = blocks // 2
    cells = blocks * 64
    p = lax.axis_index("panel")
    a = lax.axis_index("lat")
    b = lax.axis_index("lon")
    me = a * n_lon + b
    own = pl.ds(TOP, 128)

    def dev(panel, lat, lon):
        return {"panel": panel, "lat": lat, "lon": lon}

    load_f = pltpu.make_async_copy(fields_ref.at[0], fld, in_sem.at[0])
    load_v = pltpu.make_async_copy(visc_ref.at[0], va.at[:, own, :], in_sem.at[1])
    load_f.start()
    load_v.start()
    targets = (
        me,
        jnp.maximum(a - 1, 0) * n_lon + b,
        jnp.minimum(a + 1, n_lat - 1) * n_lon + b,
        a * n_lon + jnp.maximum(b - 1, 0),
        a * n_lon + jnp.minimum(b + 1, n_lon - 1),
    )
    load_o = [
        pltpu.make_async_copy(oper_ref.at[t], opr.at[i], op_sem.at[i])
        for i, t in enumerate(targets)
    ]
    for c in load_o:
        c.start()

    barrier = pltpu.get_barrier_semaphore()

    def greet(i, carry):
        t = lax.rem(me + i, ndev)
        pl.semaphore_signal(
            barrier, inc=1, device_id=dev(p, t // n_lon, lax.rem(t, n_lon)), device_id_type=MESH
        )
        return carry

    lax.fori_loop(1, ndev, greet, 0)

    def greet_other(i, carry):
        pl.semaphore_signal(barrier, inc=1, device_id=dev(1 - p, a, i), device_id_type=MESH)
        return carry

    lax.fori_loop(0, n_lon, greet_other, 0)

    lane8 = lax.broadcasted_iota(jnp.int32, (8, 128), 1)
    sub8 = lax.broadcasted_iota(jnp.int32, (8, 128), 0)
    half = lane8 // 64
    pv = jnp.broadcast_to(partner_ref[0, 0], (blocks, 128))
    block_id = lax.broadcasted_iota(jnp.int32, (blocks, 128), 0)
    before = jnp.zeros((blocks, 128), jnp.int32)
    for k in range(blocks):
        before = before + jnp.where((pv == pv[k : k + 1]) & (block_id > k), 1, 0)
    slot = pv * 2 + before
    keys, keys_r, tiles, tiles_r = [], [], [], []
    for j in range(pairs):
        s0 = jnp.broadcast_to(slot[2 * j : 2 * j + 1], (8, 128))
        s1 = jnp.broadcast_to(slot[2 * j + 1 : 2 * j + 2], (8, 128))
        key = jnp.where(half == 0, s0, s1)
        at = pl.ds(128 * j, 128)
        rr = jnp.broadcast_to(row_ref[0, :, at], (8, 128))
        cc = jnp.broadcast_to(col_ref[0, :, at], (8, 128))
        ww = jnp.broadcast_to(wid_ref[0, :, at], (8, 128))
        tile = jnp.where(sub8 == 0, rr, jnp.where(sub8 == 1, cc, ww))
        keys.append(key)
        tiles.append(tile)
        keys_r.append(pltpu.roll(key, 64, 1))
        tiles_r.append(pltpu.roll(tile, 64, 1))
    for q in range(n_lon):
        want = 2 * q + half
        acc = jnp.zeros((8, 128), jnp.int32)
        for j in range(pairs):
            acc = jnp.where(keys[j] == want, tiles[j], acc)
            acc = jnp.where(keys_r[j] == want, tiles_r[j], acc)
        ask[q] = acc

    pl.semaphore_wait(barrier, ndev - 1 + n_lon)

    def ask_copy(q, there):
        return pltpu.make_async_remote_copy(
            src_ref=ask.at[q], dst_ref=asked.at[there],
            send_sem=ask_send.at[q], recv_sem=ask_recv.at[there],
            device_id=dev(1 - p, a, q), device_id_type=MESH,
        )

    def send_ask(i, carry):
        q = lax.rem(b + i, n_lon)
        ask_copy(q, b).start()
        return carry

    lax.fori_loop(0, n_lon, send_ask, 0)

    ways = [(da, db) for da in (-1, 0, 1) for db in (-1, 0, 1) if (da, db) != (0, 0)]

    def exists(da, db):
        ok = None
        for pos, d, n in ((a, da, n_lat), (b, db, n_lon)):
            if d:
                c = (pos > 0) if d < 0 else (pos < n - 1)
                ok = c if ok is None else jnp.logical_and(ok, c)
        return ok

    def halo_copy(w, body, packed, from_left, from_right, send, recv):
        da, db = ways[w]
        src_rows = {-1: pl.ds(0, TOP), 0: pl.ds(0, 128), 1: pl.ds(128 - TOP, TOP)}[da]
        dst_rows = {-1: pl.ds(TOP + 128, TOP), 0: own, 1: pl.ds(0, TOP)}[da]
        if db == 0:
            src = body.at[:, pl.ds(TOP if da < 0 else 128, TOP), :]
            dst = body.at[:, dst_rows, :]
        else:
            src = packed.at[src_rows, :]
            dst = (from_left if db > 0 else from_right).at[dst_rows, :]
        return pltpu.make_async_remote_copy(
            src_ref=src, dst_ref=dst, send_sem=send.at[w], recv_sem=recv.at[w],
            device_id=dev(p, a + da, b + db), device_id_type=MESH,
        )

    def halo_send_all(*args):
        for w in range(8):
            @pl.when(exists(*ways[w]))
            def _(w=w):
                halo_copy(w, *args).start()

    def halo_wait_recv(*args):
        for w in range(8):
            da, db = ways[w]

            @pl.when(exists(-da, -db))
            def _(w=w):
                halo_copy(w, *args).wait_recv()

    def halo_wait_send(*args):
        for w in range(8):
            @pl.when(exists(*ways[w]))
            def _(w=w):
                halo_copy(w, *args).wait_send()

    def halo_clear(body, from_left, from_right):
        for w in range(8):
            da, db = ways[w]
            dst_rows = {-1: pl.ds(TOP + 128, TOP), 0: own, 1: pl.ds(0, TOP)}[da]

            @pl.when(jnp.logical_not(exists(-da, -db)))
            def _(da=da, db=db, dst_rows=dst_rows):
                if db == 0:
                    body[:, dst_rows, :] = jnp.zeros((body.shape[0], TOP, 128), F32)
                else:
                    buf = from_left if db > 0 else from_right
                    n = 128 if da == 0 else TOP
                    buf[dst_rows, :] = jnp.zeros((n, 128), F32)

    lane = lax.broadcasted_iota(jnp.int32, (rows_ext, 128), 1)
    lane_o = lax.broadcasted_iota(jnp.int32, (128, 128), 1)
    row_e = lax.broadcasted_iota(jnp.int32, (rows_ext, 128), 0)

    vargs = (va, vpk, vpl, vpr, v_send, v_recv)
    xargs = (x, pk, pkl, pkr, halo_send, halo_recv)
    halo_clear(va, vpl, vpr)
    load_v.wait()
    vpk[...] = pack([va[k, own, :] for k in range(levels)], visc_windows(levels), lane_o)
    halo_send_all(*vargs)
    halo_clear(x, pkl, pkr)

    load_f.wait()
    for f in range(6):
        v = fld[f].reshape(levels * 128, 128)
        hi = v.astype(BF16)
        lo = (v - hi.astype(F32)).astype(BF16)
        fcat[f, :, 0:128] = hi
        fcat[f, :, 128:256] = lo

    def rep_copy(q, there):
        return pltpu.make_async_remote_copy(
            src_ref=reply.at[q], dst_ref=answer.at[there],
            send_sem=rep_send.at[q], recv_sem=rep_recv.at[there],
            device_id=dev(1 - p, a, q), device_id_type=MESH,
        )

    sub_c = lax.broadcasted_iota(jnp.int32, (128, 256), 0)

    def serve(i, carry):
        pr = lax.rem(b // 2 + i, n_lon // 2)
        q0 = 2 * pr
        ask_copy(0, q0).wait_recv()
        ask_copy(0, q0 + 1).wait_recv()
        r0 = asked[q0]
        r1 = asked[q0 + 1]
        rr = jnp.concatenate([r0[0:1], r1[0:1]], axis=1)
        cc = jnp.concatenate([r0[1:2], r1[1:2]], axis=1)
        ww = jnp.concatenate([r0[2:3], r1[2:3]], axis=1)
        fa = ((ww >> 3).astype(F32) + 0.5) / WQ
        fo = ((ww & 7).astype(F32) + 0.5) / WQ
        cw = jnp.where(sub_c == cc, 1.0 - fo, jnp.where(sub_c == cc + 1, fo, 0.0)).astype(BF16)
        rw = jnp.where(sub_c == rr, 1.0 - fa, jnp.where(sub_c == rr + 1, fa, 0.0))
        cw2 = jnp.concatenate([cw, cw], axis=0)
        parts = []
        for f in range(6):
            g = jnp.dot(fcat[f], cw2, preferred_element_type=F32)
            parts.append(jnp.sum(g.reshape(levels, 128, 256) * rw[None], axis=1))
        res = jnp.concatenate(parts, axis=0)
        reply[q0] = res[:, 0:128]
        reply[q0 + 1] = res[:, 128:256]
        rep_copy(q0, b).start()
        rep_copy(q0 + 1, b).start()
        return carry

    lax.fori_loop(0, n_lon // 2, serve, 0)

    dest = dest_ref[0]
    sub_d = lax.broadcasted_iota(jnp.int32, (128, cells), 0)
    rm = jnp.where(sub_d == dest // 128, 1.0, 0.0).astype(BF16)
    cm = jnp.where(sub_d == dest % 128, 1.0, 0.0).astype(BF16)
    rmask[...] = rm
    cmask[:, 0:cells] = cm
    cmask[:, cells : 2 * cells] = cm
    nt = (((1,), (1,)), ((), ()))
    hit_s[...] = lax.dot_general(rm, cm, nt, preferred_element_type=F32)
    cos_a = jnp.cos(ang_ref[0])
    sin_a = jnp.sin(ang_ref[0])
    colat = math.pi / 4.0 + ((a * 128 + row_e - TOP).astype(F32) + 0.5) * (
        math.pi / 2.0
    ) / (n_lat * 128)
    inv = 1.0 / jnp.sin(colat)
    gain = inv * inv
    inv_s[...] = inv
    gain_s[...] = gain
    is_own = (row_e >= TOP) & (row_e < TOP + 128)
    edge_lane = (lane == 0) | (lane == 127)
    ca = 2.0 + 2.0 * gain
    ca = ca - jnp.where((row_e == TOP) | (row_e == TOP + 127), 1.0, 0.0)
    ca = ca - jnp.where(edge_lane, gain, 0.0)
    rim = jnp.where((row_e == TOP - 1) | (row_e == TOP + 128), 1.0, 0.0)
    coef_a[...] = jnp.where(is_own, ca, rim)
    coef_h[...] = jnp.where(is_own & edge_lane, gain, 0.0)
    halo_wait_recv(*vargs)
    vmerged = jnp.where(right_part(visc_windows(levels), lane), vpr[...], vpl[...])
    for k in range(levels):
        vh[k] = unpack(vmerged, visc_windows(levels)[k], lane)

    def wait_rep(q, carry):
        rep_copy(0, q).wait_recv()
        return carry

    lax.fori_loop(0, n_lon, wait_rep, 0)
    got = [answer[q] for q in range(n_lon)]
    got_r = [pltpu.roll(g, 64, 1) for g in got]
    half_row = half[0:1]
    picked = []
    for j in range(pairs):
        key = keys[j][0:1]
        acc = jnp.zeros((channels, 128), F32)
        for q in range(n_lon):
            acc = jnp.where(key == 2 * q + half_row, got[q], acc)
            acc = jnp.where(key == 2 * q + 1 - half_row, got_r[q], acc)
        picked.append(acc)
    values = jnp.concatenate(picked, axis=1)
    fv = [values[f * levels : (f + 1) * levels] for f in range(6)]
    turned = [
        fv[0],
        cos_a * fv[1] + sin_a * fv[2],
        cos_a * fv[2] - sin_a * fv[1],
        fv[3],
        cos_a * fv[4] + sin_a * fv[5],
        cos_a * fv[5] - sin_a * fv[4],
    ]
    hit = hit_s[...] > 0.5
    for f in range(6):
        hi = turned[f].astype(BF16)
        lo = (turned[f] - hi.astype(F32)).astype(BF16)
        left = []
        for k in range(levels):
            left.append(
                jnp.concatenate(
                    [rmask[...] * hi[k : k + 1], rmask[...] * lo[k : k + 1]], axis=1
                )
            )
        put = lax.dot_general(
            jnp.concatenate(left, axis=0), cmask[...], nt, preferred_element_type=F32
        )
        for k in range(levels):
            x[f * levels + k, own, :] = jnp.where(
                hit, put[k * 128 : (k + 1) * 128], fld[f, k]
            )

    spans = windows(levels)
    pk[...] = pack([x[c, own, :] for c in range(channels)], spans, lane_o)
    halo_send_all(*xargs)
    halo_wait_recv(*xargs)
    merged = jnp.where(right_part(spans, lane), pkr[...], pkl[...])
    for c in range(channels):
        hx[c] = unpack(merged, spans[c], lane)

    rows_ok = ((row_e >= TOP) | (a > 0)) & ((row_e < TOP + 128) | (a < n_lat - 1))
    lanes_ok = ((lane >= 64) | (b < n_lon - 1)) & ((lane < 64) | (b > 0))
    halo_ok = rows_ok & lanes_ok
    first, last = lane == 0, lane == 127

    def sides(body, rim):
        ra, rh = pltpu.roll(body, 127, 1), pltpu.roll(rim, 127, 1)
        la, lh = pltpu.roll(body, 1, 1), pltpu.roll(rim, 1, 1)
        return (
            jnp.where(last, rh, ra), jnp.where(first, lh, la),
            jnp.where(last, ra, rh), jnp.where(first, la, lh),
        )

    def next_row(v):
        return pltpu.roll(v, rows_ext - 1, 0)

    def prev_row(v):
        return pltpu.roll(v, 1, 0)

    def levels_sum(ref, base, k, index=slice(None)):
        total = None
        for d in (-1, 1):
            if 0 <= k + d < levels:
                v = ref[base + k + d, index, :]
                total = v if total is None else total + v
        return total

    def levels_diff(ref, base, k, index=slice(None)):
        up = ref[base + k + 1, index, :] if k + 1 < levels else 0.0
        down = ref[base + k - 1, index, :] if k > 0 else 0.0
        return up - down

    gain = gain_s[...]
    for f in range(3):
        for k in range(levels):
            c = f * levels + k
            body, rim = x[c], hx[c]
            r, l, rr, ll = sides(body, rim)
            mid = 4.0 + 2.0 * gain
            lap = next_row(body) + prev_row(body) + gain * (r + l) - mid * body
            lap = lap + levels_sum(x, f * levels, k)
            new = body + va[k] * lap
            lap_h = next_row(rim) + prev_row(rim) + gain * (rr + ll) - mid * rim
            lap_h = lap_h + levels_sum(hx, f * levels, k)
            new_h = rim + vh[k] * lap_h
            if f == 0:
                new = new + BUOYANCY * x[3 * levels + k]
                new_h = new_h + BUOYANCY * hx[3 * levels + k]
            st[c] = jnp.where(rows_ok, new, 0.0)
            sth[c] = jnp.where(halo_ok, new_h, 0.0)

    scale = -0.5 / (4.0 + 2.0 * gain)
    for k in range(levels):
        r, l, rr, ll = sides(st[2 * levels + k], sth[2 * levels + k])
        b1, h1 = st[levels + k], sth[levels + k]
        d = next_row(b1) - prev_row(b1) + inv_s[...] * (r - l) + levels_diff(st, 0, k)
        dh = next_row(h1) - prev_row(h1) + inv_s[...] * (rr - ll) + levels_diff(sth, 0, k)
        p1[k] = jnp.where(rows_ok, scale * d, 0.0)
        p1h[k] = jnp.where(halo_ok, scale * dh, 0.0)

    place = sub8 * 128 + lane8
    tile = jnp.zeros((8, 128), F32)
    for k in range(levels):
        part = coef_a[...] * p1[k] + coef_h[...] * p1h[k]
        part = part + jnp.where(is_own, levels_sum(p1, 0, k), 0.0)
        total = jnp.sum(jnp.sum(part, axis=0, keepdims=True), axis=1, keepdims=True)
        tile = tile + jnp.where(place == me * levels + k, total * (1.0 / 128.0), 0.0)
    mine[...] = tile

    def sum_copy(t, there, i):
        return pltpu.make_async_remote_copy(
            src_ref=mine, dst_ref=sums.at[there],
            send_sem=sum_send.at[i], recv_sem=sum_recv.at[there],
            device_id=dev(p, t // n_lon, lax.rem(t, n_lon)), device_id_type=MESH,
        )

    def send_sum(i, carry):
        sum_copy(lax.rem(me + i, ndev), me, i).start()
        return carry

    lax.fori_loop(1, ndev, send_sum, 0)

    gain_o = gain_s[own, :]
    inv_o = inv_s[own, :]
    first_o, last_o = lane_o == 0, lane_o == 127

    def sides_own(body, rim):
        r = jnp.where(last_o, pltpu.roll(rim, 127, 1), pltpu.roll(body, 127, 1))
        l = jnp.where(first_o, pltpu.roll(rim, 1, 1), pltpu.roll(body, 1, 1))
        return r, l

    for f in range(3, 6):
        for k in range(levels):
            c = f * levels + k
            body = x[c]
            mid = body[TOP : TOP + 128]
            r, l = sides_own(mid, hx[c, own, :])
            lap = next_row(body)[TOP : TOP + 128] + prev_row(body)[TOP : TOP + 128]
            lap = lap + gain_o * (r + l) - (4.0 + 2.0 * gain_o) * mid
            lap = lap + levels_sum(x, f * levels, k, own)
            onew[f, k] = mid + va[k, own, :] * lap
    store_late = pltpu.make_async_copy(
        onew.at[pl.ds(3, 3)], out_ref.at[0, pl.ds(3, 3)], out_sem.at[0]
    )
    store_late.start()
    for k in range(levels):
        body = p1[k]
        mid = body[TOP : TOP + 128]
        r, l = sides_own(mid, p1h[k, own, :])
        diff = next_row(body)[TOP : TOP + 128] - prev_row(body)[TOP : TOP + 128]
        onew[0, k] = st[k, own, :] - 0.5 * levels_diff(p1, 0, k, own)
        onew[1, k] = st[levels + k, own, :] - 0.5 * diff
        onew[2, k] = st[2 * levels + k, own, :] - 0.5 * inv_o * (r - l)

    for c in load_o:
        c.wait()

    def take_sum(i, total):
        s = lax.rem(me + i, ndev)
        sum_copy(me, s, 0).wait_recv()
        return total + sums[s]

    vec = lax.fori_loop(1, ndev, take_sum, mine[...])

    def coarse(t, k):
        prod = opr[t, k] * vec
        return jnp.sum(jnp.sum(prod, axis=0, keepdims=True), axis=1, keepdims=True)

    zero = jnp.zeros((1, 1), F32)
    mid_c = [coarse(0, k) for k in range(levels)]
    row_o = lax.broadcasted_iota(jnp.int32, (128, 128), 0)
    for k in range(levels):
        up = jnp.where(a > 0, coarse(1, k), zero)
        down = jnp.where(a < n_lat - 1, coarse(2, k), zero)
        west = jnp.where(b > 0, coarse(3, k), zero)
        east = jnp.where(b < n_lon - 1, coarse(4, k), zero)
        c = mid_c[k]
        opress[k] = p1[k, own, :] + c
        high = mid_c[k + 1] if k + 1 < levels else zero
        low = mid_c[k - 1] if k > 0 else zero
        onew[0, k] = onew[0, k] - 0.5 * (high - low)
        fix = jnp.where(row_o == 0, c - up, 0.0) + jnp.where(row_o == 127, down - c, 0.0)
        onew[1, k] = onew[1, k] - 0.5 * fix
        fix = jnp.where(first_o, c - west, 0.0) + jnp.where(last_o, east - c, 0.0)
        onew[2, k] = onew[2, k] - 0.5 * inv_o * fix
    store_new = pltpu.make_async_copy(
        onew.at[pl.ds(0, 3)], out_ref.at[0, pl.ds(0, 3)], out_sem.at[1]
    )
    store_p = pltpu.make_async_copy(opress, press_ref.at[0], out_sem.at[2])
    store_new.start()
    store_p.start()

    def end_lon(q, carry):
        ask_copy(q, b).wait_send()
        rep_copy(q, b).wait_send()
        return carry

    lax.fori_loop(0, n_lon, end_lon, 0)
    halo_wait_send(*vargs)
    halo_wait_send(*xargs)

    def end_sum(i, carry):
        sum_copy(me, me, i).wait_send()
        return carry

    lax.fori_loop(1, ndev, end_sum, 0)
    store_late.wait()
    store_new.wait()
    store_p.wait()


def solution(mesh):
    n_lat, n_lon = mesh.shape["lat"], mesh.shape["lon"]

    def shards(fields, viscosity, partner, src_row, src_col, weight_id, border_angle, dest_cell):
        levels = fields.shape[2]
        blocks = partner.shape[2]
        channels = 6 * levels
        ext = 128 + 2 * TOP
        ndev = n_lat * n_lon
        cells = src_row.shape[2]
        oper = jnp.asarray(coarse_operator(levels, n_lat, n_lon))
        vm = pl.BlockSpec(memory_space=pltpu.VMEM)
        anyw = pl.BlockSpec(memory_space=pl.ANY)
        v = lambda *s: pltpu.VMEM(s, F32)
        sem = lambda n: pltpu.SemaphoreType.DMA((n,))
        return pl.pallas_call(
            functools.partial(kernel, (n_lat, n_lon, levels, blocks)),
            out_shape=(
                jax.ShapeDtypeStruct(fields.shape, F32),
                jax.ShapeDtypeStruct(viscosity.shape, F32),
            ),
            in_specs=[vm] * 6 + [anyw] * 3,
            out_specs=(anyw, anyw),
            scratch_shapes=[
                v(6, levels, 128, 128),
                pltpu.VMEM((6, levels * 128, 256), BF16),
                pltpu.VMEM((n_lon, 8, 128), jnp.int32),
                pltpu.VMEM((n_lon, 8, 128), jnp.int32),
                v(n_lon, channels, 128),
                v(n_lon, channels, 128),
                v(channels, ext, 128),
                v(channels, ext, 128),
                v(128, 128), v(ext, 128), v(ext, 128),
                v(levels, ext, 128), v(levels, ext, 128),
                v(128, 128), v(ext, 128), v(ext, 128),
                v(ext, 128), v(ext, 128), v(ext, 128), v(ext, 128),
                v(3 * levels, ext, 128), v(3 * levels, ext, 128),
                v(levels, ext, 128), v(levels, ext, 128),
                v(128, 128),
                pltpu.VMEM((128, cells), BF16),
                pltpu.VMEM((128, 2 * cells), BF16),
                v(5, levels, 8, 128),
                v(ndev, 8, 128),
                v(8, 128),
                v(6, levels, 128, 128),
                v(levels, 128, 128),
                sem(2), sem(5), sem(3),
                sem(n_lon), sem(n_lon), sem(n_lon), sem(n_lon),
                sem(8), sem(8), sem(8), sem(8), sem(ndev), sem(ndev),
            ],
            compiler_params=pltpu.CompilerParams(
                collective_id=0, has_side_effects=True, vmem_limit_bytes=48 * 1024 * 1024
            ),
            name="shell_step",
        )(
            partner, src_row, src_col, weight_id, border_angle, dest_cell,
            fields, viscosity, oper,
        )

    return jax.shard_map(
        shards,
        mesh=mesh,
        in_specs=(
            P("panel", None, None, "lat", "lon"),
            P("panel", None, "lat", "lon"),
            P("panel", "lat", "lon", None),
            P("panel", "lat", "lon"),
            P("panel", "lat", "lon"),
            P("panel", "lat", "lon"),
            P("panel", "lat", "lon"),
            P("panel", "lat", "lon"),
        ),
        out_specs=(P("panel", None, None, "lat", "lon"), P("panel", None, "lat", "lon")),
        check_vma=False,
    )
```

time: 210 us -> 40.3 us (0.19); the launches traced: 206 us -> 39.9 us
  local copies, waits for them, and re-layouts: 73.7 us -> 9.29 us
  starting transfers between devices: 55.8 us -> 0 us
  Pallas kernels: 0 us -> 30 us
  waiting for transfers between devices: 28.1 us -> 0 us
  blocking collectives: 26.1 us -> 0 us
  other arithmetic: 19.7 us -> 0 us
    ppermute x18 -> x0, starting transfers between devices: 45.3 us -> none  [the longest x8 30.5 us: padded_2(): before = lax.ppermute(last, axis, up)]
    pallas_call x0 -> x1, Pallas kernels: none -> 30 us  [shards(): pl.pallas_call(functools.partial(kernel, (n_lat, n_lon, levels, blocks)),...]
    all_gather x1 -> x0, blocking collectives: 26.1 us -> none  [shards(): lax.all_gather(block_sum[:, None], ('lat', 'lon'), axis=1, tiled=True)]
    gather x9 -> x0, local copies, waits for them, and re-layouts: 26 us -> none  [the longest x8 25.4 us: shards(): jnp.take(flat_cells, requests + offset, axis=1)]
    ppermute x18 -> x0, waiting for transfers between devices: 17 us -> none  [the longest x2 10.7 us: partner_2(): return lax.ppermute(block, axis, route)]
    scatter x3 -> x0, local copies, waits for them, and re-layouts: 14 us -> none  [the longest x2 13.4 us: shards(): flat_cells.at[:, dest_cell[0, 0]].set(rotated)]
    slice x22 -> x0, local copies, waits for them, and re-layouts: 13 us -> none  [the longest x6 8.6 us: padded_2(): leading = lax.slice_in_dim(shard, 0, width, axis=dim)]
    all_to_all x2 -> x0, waiting for transfers between devices: 11.1 us -> none  [the longest x1 11.1 us: shards(): lax.all_to_all(served, 'lon', split_axis=2, concat_axis=2, tiled=True)]
  transfers between devices with their start and end apart: 20 -> 0, of which waited for: 9 -> 0; matrix products, arithmetic and copies ran while one was open for 14% -> 0% of each run, Pallas kernels for 0% -> 0%
where the time goes in v1:
time: 40.3 us; the launch traced here: 39.9 us
  Pallas kernels  30 us (74%)
  local copies, waits for them, and re-layouts  9.29 us (23%)
  between operations  0.65 us (2%)
    pallas_call x1, Pallas kernels, shards(): pl.pallas_call(functools.partial(kernel, (n_lat, n_lon, levels, blocks)),...  30 us
    unnamed x19, local copies, waits for them, and re-layouts  9.29 us

profile of v1, /device:TPU:0, one launch (start us, length us, event | category | flops | bytes accessed | tf_op | source)
XLA Modules:
  0.0 39.9 jit_solution(9350505596435340972)
XLA Ops:
  0.6 0.7 %copy.11.partner_ref = s32[1,1,8,1]{3,2,1,0:T(8,128)S(1)} copy(s32[1,1,8,1]{2,3,1,0:T(1,128)} %param.11) | data formatting | bytes 64 | tf_op args[2]
  1.4 0.0 copy-start
  1.4 1.4 %copy-done = f32[1,6,4,128,128]{4,3,2,1,0:T(8,128)S(1)} copy-done((f32[1,6,4,128,128]{4,3,2,1,0:T(8,128)S(1)}, f32[1,6,4,128,128]{4,3,2,1,0:T(8,128)}, u32[]{:S(2)}) %copy-start) | copy-done | bytes 1572888
  2.8 0.0 copy-start.1
  2.8 0.9 %copy-done.1 = f32[1,4,128,128]{3,2,1,0:T(8,128)S(1)} copy-done((f32[1,4,128,128]{3,2,1,0:T(8,128)S(1)}, f32[1,4,128,128]{3,2,1,0:T(8,128)}, u32[]{:S(2)}) %copy-start.1) | copy-done | bytes 262168
  3.7 0.0 copy-start.2
  3.7 0.9 %copy-done.2 = f32[16,4,8,128]{3,2,1,0:T(8,128)S(1)} copy-done((f32[16,4,8,128]{3,2,1,0:T(8,128)S(1)}, f32[16,4,8,128]{3,2,1,0:T(8,128)}, u32[]{:S(2)}) %copy-start.2) | copy-done | bytes 262168
  4.7 0.0 copy-start.3
  4.7 0.7 %copy-done.3 = s32[1,1,512]{2,1,0:T(1,128)S(1)} copy-done((s32[1,1,512]{2,1,0:T(1,128)S(1)}, s32[1,1,512]{2,1,0:T(1,128)}, u32[]{:S(2)}) %copy-start.3) | copy-done | bytes 2072
  5.4 0.0 copy-start.4
  5.4 0.7 %copy-done.4 = s32[1,1,512]{2,1,0:T(1,128)S(1)} copy-done((s32[1,1,512]{2,1,0:T(1,128)S(1)}, s32[1,1,512]{2,1,0:T(1,128)}, u32[]{:S(2)}) %copy-start.4) | copy-done | bytes 2072
  6.0 0.0 copy-start.5
  6.0 0.7 %copy-done.5 = s32[1,1,512]{2,1,0:T(1,128)S(1)} copy-done((s32[1,1,512]{2,1,0:T(1,128)S(1)}, s32[1,1,512]{2,1,0:T(1,128)}, u32[]{:S(2)}) %copy-start.5) | copy-done | bytes 2072
  6.7 0.0 copy-start.6
  6.7 0.7 %copy-done.6 = f32[1,1,512]{2,1,0:T(1,128)S(1)} copy-done((f32[1,1,512]{2,1,0:T(1,128)S(1)}, f32[1,1,512]{2,1,0:T(1,128)}, u32[]{:S(2)}) %copy-start.6) | copy-done | bytes 2072
  7.4 0.0 copy-start.7
  7.4 0.7 %copy-done.7 = s32[1,1,512]{2,1,0:T(1,128)S(1)} copy-done((s32[1,1,512]{2,1,0:T(1,128)S(1)}, s32[1,1,512]{2,1,0:T(1,128)}, u32[]{:S(2)}) %copy-start.7) | copy-done | bytes 2072
  8.1 30.0 %shell_step.1 = (f32[1,6,4,128,128]{4,3,2,1,0:T(8,128)S(1)}, f32[1,4,128,128]{3,2,1,0:T(8,128)S(1)}) custom-call(s32[1,1,8,1]{3,2,1,0:T(8,128)S(1)} %copy.11.partner_ref, s32[1,1,512]{2,1,0:T(1,128)S(1)} %copy-done.3, s32[1,1,512]{2,1,0:T(1,128)S(1)} %copy-done.4, s32[1,1,512]{2,1,0:T(1,128)S(1)} %copy-done.5, f32[1,1,512]{2,1,0:T(1,128)S(1)} %copy-done.6, ...), custom_call_target="tpu_custom_call" | custom-call | tf_op jit(solution)/shard_map/shell_step/pallas_call | solution.py:569
  38.1 1.1 %copy.14 = f32[1,6,4,128,128]{4,3,2,1,0:T(8,128)} copy(f32[1,6,4,128,128]{4,3,2,1,0:T(8,128)S(1)} %get-tuple-element.4) | data formatting | bytes 3145728
  39.2 0.7 %copy.15 = f32[1,4,128,128]{3,2,1,0:T(8,128)} copy(f32[1,4,128,128]{3,2,1,0:T(8,128)S(1)} %get-tuple-element.5) | data formatting | bytes 524288
Async XLA Ops:
  1.4 1.4 %copy-start = (f32[1,6,4,128,128]{4,3,2,1,0:T(8,128)S(1)}, f32[1,6,4,128,128]{4,3,2,1,0:T(8,128)}, u32[]{:S(2)}) copy-start(f32[1,6,4,128,128]{4,3,2,1,0:T(8,128)} %fields_ref.1) | copy-start | bytes 4718596
  2.8 0.9 %copy-start.1 = (f32[1,4,128,128]{3,2,1,0:T(8,128)S(1)}, f32[1,4,128,128]{3,2,1,0:T(8,128)}, u32[]{:S(2)}) copy-start(f32[1,4,128,128]{3,2,1,0:T(8,128)} %visc_ref.1) | copy-start | bytes 786436
  3.7 0.9 %copy-start.2 = (f32[16,4,8,128]{3,2,1,0:T(8,128)S(1)}, f32[16,4,8,128]{3,2,1,0:T(8,128)}, u32[]{:S(2)}) copy-start(f32[16,4,8,128]{3,2,1,0:T(8,128)} %constant.2.clone.oper_ref) | copy-start | bytes 786436
  4.7 0.7 %copy-start.3 = (s32[1,1,512]{2,1,0:T(1,128)S(1)}, s32[1,1,512]{2,1,0:T(1,128)}, u32[]{:S(2)}) copy-start(s32[1,1,512]{2,1,0:T(1,128)} %row_ref.1) | copy-start | bytes 6148
  5.4 0.7 %copy-start.4 = (s32[1,1,512]{2,1,0:T(1,128)S(1)}, s32[1,1,512]{2,1,0:T(1,128)}, u32[]{:S(2)}) copy-start(s32[1,1,512]{2,1,0:T(1,128)} %col_ref.1) | copy-start | bytes 6148
  6.0 0.7 %copy-start.5 = (s32[1,1,512]{2,1,0:T(1,128)S(1)}, s32[1,1,512]{2,1,0:T(1,128)}, u32[]{:S(2)}) copy-start(s32[1,1,512]{2,1,0:T(1,128)} %wid_ref.1) | copy-start | bytes 6148
  6.7 0.7 %copy-start.6 = (f32[1,1,512]{2,1,0:T(1,128)S(1)}, f32[1,1,512]{2,1,0:T(1,128)}, u32[]{:S(2)}) copy-start(f32[1,1,512]{2,1,0:T(1,128)} %ang_ref.1) | copy-start | bytes 6148
  7.4 0.7 %copy-start.7 = (s32[1,1,512]{2,1,0:T(1,128)S(1)}, s32[1,1,512]{2,1,0:T(1,128)}, u32[]{:S(2)}) copy-start(s32[1,1,512]{2,1,0:T(1,128)} %dest_ref.1) | copy-start | bytes 6148

commit v2 on v1

--- a/solution.py
+++ b/solution.py
@@ -33,14 +33,19 @@
     q = np.einsum("ax,oy,rz->aorxyz", qa, qo, qr).reshape(inv.size, inv.size)
     full = (q.T * inv.reshape(-1)) @ q / math.sqrt(n_lat * n_lon)
     count = inv.size
-    wide = np.zeros((count, 8 * 128), np.float32)
+    used = -(-count // 128)
+    wide = np.zeros((count, used * 128), np.float32)
     wide[:, :count] = full
-    return wide.reshape(n_lat * n_lon, levels, 8, 128)
-
-
-def windows(levels):
+    return wide.reshape(n_lat * n_lon, levels, used, 128)
+
+
+GROUPS = ((0, 4), (4, 6))
+WIDTHS = (3, 3, 3, 2, 1, 1)
+
+
+def windows(levels, group):
     spans, at = [], 0
-    for width in (3, 3, 3, 2, 1, 1):
+    for width in WIDTHS[group[0] : group[1]]:
         for _ in range(levels):
             spans.append((at + width, width))
             at += 2 * width
@@ -75,13 +80,16 @@
 
 def kernel(
     dims,
-    partner_ref, row_ref, col_ref, wid_ref, ang_ref, dest_ref, fields_ref, visc_ref, oper_ref,
+    partner_in, row_in, col_in, wid_in, ang_in, dest_in, fields_ref, visc_ref, oper_ref,
     out_ref, press_ref,
-    fld, fcat, ask, asked, reply, answer, x, hx, pk, pkl, pkr, va, vh, vpk, vpl, vpr,
+    partner_ref, row_ref, col_ref, wid_ref, ang_ref, dest_ref,
+    fld, fcat, ask, asked, reply0, answer0, reply1, answer1, x, hx,
+    pk, pkl, pkr, pk2, pkl2, pkr2, to_up, to_dn, from_up, from_dn,
+    to_up2, to_dn2, from_up2, from_dn2, va, vh, vpk, vpl, vpr,
     inv_s, gain_s, coef_a, coef_h, st, sth, p1, p1h, hit_s, rmask, cmask,
     opr, sums, mine, onew, opress,
     in_sem, op_sem, out_sem, ask_send, ask_recv, rep_send, rep_recv,
-    halo_send, halo_recv, v_send, v_recv, sum_send, sum_recv,
+    halo_send, halo_recv, halo2_send, halo2_recv, v_send, v_recv, sum_send, sum_recv,
 ):
     n_lat, n_lon, levels, blocks = dims
     ndev = n_lat * n_lon
@@ -100,6 +108,17 @@
 
     load_f = pltpu.make_async_copy(fields_ref.at[0], fld, in_sem.at[0])
     load_v = pltpu.make_async_copy(visc_ref.at[0], va.at[:, own, :], in_sem.at[1])
+    small = [
+        pltpu.make_async_copy(src, dst, in_sem.at[2 + i])
+        for i, (src, dst) in enumerate(
+            (
+                (partner_in, partner_ref), (row_in, row_ref), (col_in, col_ref),
+                (wid_in, wid_ref), (ang_in, ang_ref), (dest_in, dest_ref),
+            )
+        )
+    ]
+    for c in small:
+        c.start()
     load_f.start()
     load_v.start()
     targets = (
@@ -136,7 +155,17 @@
     lane8 = lax.broadcasted_iota(jnp.int32, (8, 128), 1)
     sub8 = lax.broadcasted_iota(jnp.int32, (8, 128), 0)
     half = lane8 // 64
-    pv = jnp.broadcast_to(partner_ref[0, 0], (blocks, 128))
+    zero_rows = jnp.zeros((6 * levels, TOP, 128), F32)
+    x[:, 0:TOP, :] = zero_rows
+    x[:, TOP + 128 : rows_ext, :] = zero_rows
+    for c in small[:4]:
+        c.wait()
+    named = jnp.broadcast_to(partner_ref[0], (blocks, blocks)).astype(F32)
+    diag = lax.broadcasted_iota(jnp.int32, (blocks, blocks), 0) == lax.broadcasted_iota(
+        jnp.int32, (blocks, blocks), 1
+    )
+    pv = jnp.sum(jnp.where(diag, named, 0.0), axis=1, keepdims=True).astype(jnp.int32)
+    pv = jnp.broadcast_to(pv, (blocks, 128))
     block_id = lax.broadcasted_iota(jnp.int32, (blocks, 128), 0)
     before = jnp.zeros((blocks, 128), jnp.int32)
     for k in range(blocks):
@@ -162,7 +191,7 @@
         for j in range(pairs):
             acc = jnp.where(keys[j] == want, tiles[j], acc)
             acc = jnp.where(keys_r[j] == want, tiles_r[j], acc)
-        ask[q] = acc
+        ask[q] = acc[0:4]
 
     pl.semaphore_wait(barrier, ndev - 1 + n_lon)
 
@@ -190,66 +219,123 @@
                 ok = c if ok is None else jnp.logical_and(ok, c)
         return ok
 
-    def halo_copy(w, body, packed, from_left, from_right, send, recv):
+    def halo_copy(w, h):
         da, db = ways[w]
         src_rows = {-1: pl.ds(0, TOP), 0: pl.ds(0, 128), 1: pl.ds(128 - TOP, TOP)}[da]
         dst_rows = {-1: pl.ds(TOP + 128, TOP), 0: own, 1: pl.ds(0, TOP)}[da]
-        if db == 0:
-            src = body.at[:, pl.ds(TOP if da < 0 else 128, TOP), :]
-            dst = body.at[:, dst_rows, :]
+        if db == 0 and h["rows"] is not None:
+            up, dn, got_up, got_dn = h["rows"]
+            src, dst = (up, got_dn) if da < 0 else (dn, got_up)
+        elif db == 0:
+            src = h["body"].at[:, pl.ds(TOP if da < 0 else 128, TOP), :]
+            dst = h["body"].at[:, dst_rows, :]
         else:
-            src = packed.at[src_rows, :]
-            dst = (from_left if db > 0 else from_right).at[dst_rows, :]
+            into = h["cols"][1 if db > 0 else 2]
+            src = h["cols"][0].at[src_rows, :]
+            dst = into if h["flat"] else into.at[dst_rows, :]
         return pltpu.make_async_remote_copy(
-            src_ref=src, dst_ref=dst, send_sem=send.at[w], recv_sem=recv.at[w],
+            src_ref=src, dst_ref=dst, send_sem=h["send"].at[w], recv_sem=h["recv"].at[w],
             device_id=dev(p, a + da, b + db), device_id_type=MESH,
         )
 
-    def halo_send_all(*args):
-        for w in range(8):
+    def ways_of(h):
+        return [w for w, (da, db) in enumerate(ways) if not (h["flat"] and da and db)]
+
+    def halo_send_all(h):
+        for w in ways_of(h):
             @pl.when(exists(*ways[w]))
             def _(w=w):
-                halo_copy(w, *args).start()
-
-    def halo_wait_recv(*args):
-        for w in range(8):
+                halo_copy(w, h).start()
+
+    def halo_wait_recv(h):
+        for w in ways_of(h):
             da, db = ways[w]
 
             @pl.when(exists(-da, -db))
             def _(w=w):
-                halo_copy(w, *args).wait_recv()
-
-    def halo_wait_send(*args):
-        for w in range(8):
+                halo_copy(w, h).wait_recv()
+
+    def halo_wait_send(h):
+        for w in ways_of(h):
             @pl.when(exists(*ways[w]))
             def _(w=w):
-                halo_copy(w, *args).wait_send()
-
-    def halo_clear(body, from_left, from_right):
-        for w in range(8):
+                halo_copy(w, h).wait_send()
+
+    def halo_clear(h):
+        for w in ways_of(h):
             da, db = ways[w]
             dst_rows = {-1: pl.ds(TOP + 128, TOP), 0: own, 1: pl.ds(0, TOP)}[da]
+            if db == 0 and h["rows"] is not None:
+                continue
 
             @pl.when(jnp.logical_not(exists(-da, -db)))
             def _(da=da, db=db, dst_rows=dst_rows):
                 if db == 0:
-                    body[:, dst_rows, :] = jnp.zeros((body.shape[0], TOP, 128), F32)
+                    h["body"][:, dst_rows, :] = jnp.zeros((levels, TOP, 128), F32)
                 else:
-                    buf = from_left if db > 0 else from_right
-                    n = 128 if da == 0 else TOP
-                    buf[dst_rows, :] = jnp.zeros((n, 128), F32)
+                    buf = h["cols"][1 if db > 0 else 2]
+                    if h["flat"]:
+                        buf[...] = jnp.zeros((128, 128), F32)
+                    else:
+                        buf[dst_rows, :] = jnp.zeros((128 if da == 0 else TOP, 128), F32)
+
+    def rows_of(group):
+        spots, at = [], 0
+        for f in range(*group):
+            for k in range(levels):
+                spots.append((f * levels + k, at, WIDTHS[f]))
+                at += WIDTHS[f]
+        return spots
+
+    def pack_rows(group, h):
+        up, dn = h["rows"][0:2]
+
+        @pl.when(a > 0)
+        def _():
+            for c, at, w in rows_of(group):
+                up[at : at + w, :] = x[c, TOP : TOP + w, :]
+
+        @pl.when(a < n_lat - 1)
+        def _():
+            for c, at, w in rows_of(group):
+                dn[at : at + w, :] = x[c, TOP + 128 - w : TOP + 128, :]
+
+    def unpack_rows(group, h):
+        got_up, got_dn = h["rows"][2:4]
+
+        @pl.when(a > 0)
+        def _():
+            for c, at, w in rows_of(group):
+                x[c, TOP - w : TOP, :] = got_up[at : at + w, :]
+
+        @pl.when(a < n_lat - 1)
+        def _():
+            for c, at, w in rows_of(group):
+                x[c, TOP + 128 : TOP + 128 + w, :] = got_dn[at : at + w, :]
 
     lane = lax.broadcasted_iota(jnp.int32, (rows_ext, 128), 1)
     lane_o = lax.broadcasted_iota(jnp.int32, (128, 128), 1)
     row_e = lax.broadcasted_iota(jnp.int32, (rows_ext, 128), 0)
 
-    vargs = (va, vpk, vpl, vpr, v_send, v_recv)
-    xargs = (x, pk, pkl, pkr, halo_send, halo_recv)
-    halo_clear(va, vpl, vpr)
+    vargs = dict(
+        rows=None, body=va, cols=(vpk, vpl, vpr), flat=False, send=v_send, recv=v_recv
+    )
+    hargs = (
+        dict(
+            rows=(to_up, to_dn, from_up, from_dn), cols=(pk, pkl, pkr), flat=False,
+            send=halo_send, recv=halo_recv,
+        ),
+        dict(
+            rows=(to_up2, to_dn2, from_up2, from_dn2), cols=(pk2, pkl2, pkr2), flat=True,
+            send=halo2_send, recv=halo2_recv,
+        ),
+    )
+    halo_clear(vargs)
     load_v.wait()
     vpk[...] = pack([va[k, own, :] for k in range(levels)], visc_windows(levels), lane_o)
-    halo_send_all(*vargs)
-    halo_clear(x, pkl, pkr)
+    halo_send_all(vargs)
+    halo_clear(hargs[0])
+    halo_clear(hargs[1])
 
     load_f.wait()
     for f in range(6):
@@ -259,52 +345,7 @@
         fcat[f, :, 0:128] = hi
         fcat[f, :, 128:256] = lo
 
-    def rep_copy(q, there):
-        return pltpu.make_async_remote_copy(
-            src_ref=reply.at[q], dst_ref=answer.at[there],
-            send_sem=rep_send.at[q], recv_sem=rep_recv.at[there],
-            device_id=dev(1 - p, a, q), device_id_type=MESH,
-        )
-
-    sub_c = lax.broadcasted_iota(jnp.int32, (128, 256), 0)
-
-    def serve(i, carry):
-        pr = lax.rem(b // 2 + i, n_lon // 2)
-        q0 = 2 * pr
-        ask_copy(0, q0).wait_recv()
-        ask_copy(0, q0 + 1).wait_recv()
-        r0 = asked[q0]
-        r1 = asked[q0 + 1]
-        rr = jnp.concatenate([r0[0:1], r1[0:1]], axis=1)
-        cc = jnp.concatenate([r0[1:2], r1[1:2]], axis=1)
-        ww = jnp.concatenate([r0[2:3], r1[2:3]], axis=1)
-        fa = ((ww >> 3).astype(F32) + 0.5) / WQ
-        fo = ((ww & 7).astype(F32) + 0.5) / WQ
-        cw = jnp.where(sub_c == cc, 1.0 - fo, jnp.where(sub_c == cc + 1, fo, 0.0)).astype(BF16)
-        rw = jnp.where(sub_c == rr, 1.0 - fa, jnp.where(sub_c == rr + 1, fa, 0.0))
-        cw2 = jnp.concatenate([cw, cw], axis=0)
-        parts = []
-        for f in range(6):
-            g = jnp.dot(fcat[f], cw2, preferred_element_type=F32)
-            parts.append(jnp.sum(g.reshape(levels, 128, 256) * rw[None], axis=1))
-        res = jnp.concatenate(parts, axis=0)
-        reply[q0] = res[:, 0:128]
-        reply[q0 + 1] = res[:, 128:256]
-        rep_copy(q0, b).start()
-        rep_copy(q0 + 1, b).start()
-        return carry
-
-    lax.fori_loop(0, n_lon // 2, serve, 0)
-
-    dest = dest_ref[0]
-    sub_d = lax.broadcasted_iota(jnp.int32, (128, cells), 0)
-    rm = jnp.where(sub_d == dest // 128, 1.0, 0.0).astype(BF16)
-    cm = jnp.where(sub_d == dest % 128, 1.0, 0.0).astype(BF16)
-    rmask[...] = rm
-    cmask[:, 0:cells] = cm
-    cmask[:, cells : 2 * cells] = cm
-    nt = (((1,), (1,)), ((), ()))
-    hit_s[...] = lax.dot_general(rm, cm, nt, preferred_element_type=F32)
+    small[4].wait()
     cos_a = jnp.cos(ang_ref[0])
     sin_a = jnp.sin(ang_ref[0])
     colat = math.pi / 4.0 + ((a * 128 + row_e - TOP).astype(F32) + 0.5) * (
@@ -322,63 +363,125 @@
     rim = jnp.where((row_e == TOP - 1) | (row_e == TOP + 128), 1.0, 0.0)
     coef_a[...] = jnp.where(is_own, ca, rim)
     coef_h[...] = jnp.where(is_own & edge_lane, gain, 0.0)
-    halo_wait_recv(*vargs)
+
+    replies, answers = (reply0, reply1), (answer0, answer1)
+
+    def rep_copy(g, q, there):
+        return pltpu.make_async_remote_copy(
+            src_ref=replies[g].at[q], dst_ref=answers[g].at[there],
+            send_sem=rep_send.at[g * n_lon + q], recv_sem=rep_recv.at[g * n_lon + there],
+            device_id=dev(1 - p, a, q), device_id_type=MESH,
+        )
+
+    sub_c = lax.broadcasted_iota(jnp.int32, (128, 256), 0)
+
+    def serve(g, i, carry):
+        pr = lax.rem(b // 2 + i, n_lon // 2)
+        q0 = 2 * pr
+        if g == 0:
+            ask_copy(0, q0).wait_recv()
+            ask_copy(0, q0 + 1).wait_recv()
+        r0 = asked[q0]
+        r1 = asked[q0 + 1]
+        rr = jnp.concatenate([r0[0:1], r1[0:1]], axis=1)
+        cc = jnp.concatenate([r0[1:2], r1[1:2]], axis=1)
+        ww = jnp.concatenate([r0[2:3], r1[2:3]], axis=1)
+        fa = ((ww >> 3).astype(F32) + 0.5) / WQ
+        fo = ((ww & 7).astype(F32) + 0.5) / WQ
+        cw = jnp.where(sub_c == cc, 1.0 - fo, jnp.where(sub_c == cc + 1, fo, 0.0)).astype(BF16)
+        rw = jnp.where(sub_c == rr, 1.0 - fa, jnp.where(sub_c == rr + 1, fa, 0.0))
+        cw2 = jnp.concatenate([cw, cw], axis=0)
+        parts = []
+        for f in range(*GROUPS[g]):
+            v = jnp.dot(fcat[f], cw2, preferred_element_type=F32)
+            parts.append(jnp.sum(v.reshape(levels, 128, 256) * rw[None], axis=1))
+        res = jnp.concatenate(parts, axis=0)
+        replies[g][q0] = res[:, 0:128]
+        replies[g][q0 + 1] = res[:, 128:256]
+        rep_copy(g, q0, b).start()
+        rep_copy(g, q0 + 1, b).start()
+        return carry
+
+    lax.fori_loop(0, n_lon // 2, functools.partial(serve, 0), 0)
+    small[5].wait()
+    dest = dest_ref[0]
+    sub_d = lax.broadcasted_iota(jnp.int32, (128, cells), 0)
+    rm = jnp.where(sub_d == dest // 128, 1.0, 0.0).astype(BF16)
+    cm = jnp.where(sub_d == dest % 128, 1.0, 0.0).astype(BF16)
+    rmask[...] = rm
+    cmask[:, 0:cells] = cm
+    cmask[:, cells : 2 * cells] = cm
+    nt = (((1,), (1,)), ((), ()))
+    hit_s[...] = lax.dot_general(rm, cm, nt, preferred_element_type=F32)
+    lax.fori_loop(0, n_lon // 2, functools.partial(serve, 1), 0)
+    halo_wait_recv(vargs)
     vmerged = jnp.where(right_part(visc_windows(levels), lane), vpr[...], vpl[...])
     for k in range(levels):
         vh[k] = unpack(vmerged, visc_windows(levels)[k], lane)
 
-    def wait_rep(q, carry):
-        rep_copy(0, q).wait_recv()
-        return carry
-
-    lax.fori_loop(0, n_lon, wait_rep, 0)
-    got = [answer[q] for q in range(n_lon)]
-    got_r = [pltpu.roll(g, 64, 1) for g in got]
     half_row = half[0:1]
-    picked = []
-    for j in range(pairs):
-        key = keys[j][0:1]
-        acc = jnp.zeros((channels, 128), F32)
-        for q in range(n_lon):
-            acc = jnp.where(key == 2 * q + half_row, got[q], acc)
-            acc = jnp.where(key == 2 * q + 1 - half_row, got_r[q], acc)
-        picked.append(acc)
-    values = jnp.concatenate(picked, axis=1)
-    fv = [values[f * levels : (f + 1) * levels] for f in range(6)]
-    turned = [
-        fv[0],
-        cos_a * fv[1] + sin_a * fv[2],
-        cos_a * fv[2] - sin_a * fv[1],
-        fv[3],
-        cos_a * fv[4] + sin_a * fv[5],
-        cos_a * fv[5] - sin_a * fv[4],
-    ]
-    hit = hit_s[...] > 0.5
-    for f in range(6):
-        hi = turned[f].astype(BF16)
-        lo = (turned[f] - hi.astype(F32)).astype(BF16)
-        left = []
-        for k in range(levels):
-            left.append(
-                jnp.concatenate(
-                    [rmask[...] * hi[k : k + 1], rmask[...] * lo[k : k + 1]], axis=1
+
+    def fill(g):
+        first_f, end_f = GROUPS[g]
+
+        def wait_rep(q, carry):
+            rep_copy(g, 0, q).wait_recv()
+            return carry
+
+        lax.fori_loop(0, n_lon, wait_rep, 0)
+        got = [answers[g][q] for q in range(n_lon)]
+        got_r = [pltpu.roll(v, 64, 1) for v in got]
+        picked = []
+        for j in range(pairs):
+            key = keys[j][0:1]
+            acc = jnp.zeros(((end_f - first_f) * levels, 128), F32)
+            for q in range(n_lon):
+                acc = jnp.where(key == 2 * q + half_row, got[q], acc)
+                acc = jnp.where(key == 2 * q + 1 - half_row, got_r[q], acc)
+            picked.append(acc)
+        values = jnp.concatenate(picked, axis=1)
+        fv = [values[f * levels : (f + 1) * levels] for f in range(end_f - first_f)]
+        if g == 0:
+            turned = [
+                fv[0], cos_a * fv[1] + sin_a * fv[2], cos_a * fv[2] - sin_a * fv[1], fv[3],
+            ]
+        else:
+            turned = [cos_a * fv[0] + sin_a * fv[1], cos_a * fv[1] - sin_a * fv[0]]
+        hit = hit_s[...] > 0.5
+        for f in range(first_f, end_f):
+            v = turned[f - first_f]
+            hi = v.astype(BF16)
+            lo = (v - hi.astype(F32)).astype(BF16)
+            left = []
+            for k in range(levels):
+                left.append(
+                    jnp.concatenate(
+                        [rmask[...] * hi[k : k + 1], rmask[...] * lo[k : k + 1]], axis=1
+                    )
                 )
+            put = lax.dot_general(
+                jnp.concatenate(left, axis=0), cmask[...], nt, preferred_element_type=F32
             )
-        put = lax.dot_general(
-            jnp.concatenate(left, axis=0), cmask[...], nt, preferred_element_type=F32
-        )
-        for k in range(levels):
-            x[f * levels + k, own, :] = jnp.where(
-                hit, put[k * 128 : (k + 1) * 128], fld[f, k]
-            )
-
-    spans = windows(levels)
-    pk[...] = pack([x[c, own, :] for c in range(channels)], spans, lane_o)
-    halo_send_all(*xargs)
-    halo_wait_recv(*xargs)
+            for k in range(levels):
+                x[f * levels + k, own, :] = jnp.where(
+                    hit, put[k * 128 : (k + 1) * 128], fld[f, k]
+                )
+        h = hargs[g]
+        pack_rows(GROUPS[g], h)
+        h["cols"][0][...] = pack(
+            [x[c, own, :] for c in range(first_f * levels, end_f * levels)],
+            windows(levels, GROUPS[g]), lane_o,
+        )
+        halo_send_all(h)
+
+    fill(0)
+    fill(1)
+    halo_wait_recv(hargs[0])
+    unpack_rows(GROUPS[0], hargs[0])
+    spans = windows(levels, GROUPS[0])
     merged = jnp.where(right_part(spans, lane), pkr[...], pkl[...])
-    for c in range(channels):
-        hx[c] = unpack(merged, spans[c], lane)
+    for c, span in enumerate(spans):
+        hx[c] = unpack(merged, span, lane)
 
     rows_ok = ((row_e >= TOP) | (a > 0)) & ((row_e < TOP + 128) | (a < n_lat - 1))
     lanes_ok = ((lane >= 64) | (b < n_lon - 1)) & ((lane < 64) | (b > 0))
@@ -440,8 +543,10 @@
         p1[k] = jnp.where(rows_ok, scale * d, 0.0)
         p1h[k] = jnp.where(halo_ok, scale * dh, 0.0)
 
-    place = sub8 * 128 + lane8
-    tile = jnp.zeros((8, 128), F32)
+    shape = mine.shape
+    place = lax.broadcasted_iota(jnp.int32, shape, 0) * 128
+    place = place + lax.broadcasted_iota(jnp.int32, shape, 1)
+    tile = jnp.zeros(shape, F32)
     for k in range(levels):
         part = coef_a[...] * p1[k] + coef_h[...] * p1h[k]
         part = part + jnp.where(is_own, levels_sum(p1, 0, k), 0.0)
@@ -471,6 +576,12 @@
         l = jnp.where(first_o, pltpu.roll(rim, 1, 1), pltpu.roll(body, 1, 1))
         return r, l
 
+    halo_wait_recv(hargs[1])
+    unpack_rows(GROUPS[1], hargs[1])
+    spans = windows(levels, GROUPS[1])
+    merged = jnp.where(right_part(spans, lane_o), pkr2[...], pkl2[...])
+    for c, span in enumerate(spans):
+        hx[4 * levels + c, own, :] = unpack(merged, span, lane_o)
     for f in range(3, 6):
         for k in range(levels):
             c = f * levels + k
@@ -534,12 +645,14 @@
 
     def end_lon(q, carry):
         ask_copy(q, b).wait_send()
-        rep_copy(q, b).wait_send()
+        rep_copy(0, q, b).wait_send()
+        rep_copy(1, q, b).wait_send()
         return carry
 
     lax.fori_loop(0, n_lon, end_lon, 0)
-    halo_wait_send(*vargs)
-    halo_wait_send(*xargs)
+    halo_wait_send(vargs)
+    halo_wait_send(hargs[0])
+    halo_wait_send(hargs[1])
 
     def end_sum(i, carry):
         sum_copy(me, me, i).wait_send()
@@ -562,28 +675,34 @@
         ndev = n_lat * n_lon
         cells = src_row.shape[2]
         oper = jnp.asarray(coarse_operator(levels, n_lat, n_lon))
-        vm = pl.BlockSpec(memory_space=pltpu.VMEM)
         anyw = pl.BlockSpec(memory_space=pl.ANY)
         v = lambda *s: pltpu.VMEM(s, F32)
+        vi = lambda *s: pltpu.VMEM(s, jnp.int32)
         sem = lambda n: pltpu.SemaphoreType.DMA((n,))
+        rows0, rows1 = 11 * levels, 2 * levels
+        used = oper.shape[2]
         return pl.pallas_call(
             functools.partial(kernel, (n_lat, n_lon, levels, blocks)),
             out_shape=(
                 jax.ShapeDtypeStruct(fields.shape, F32),
                 jax.ShapeDtypeStruct(viscosity.shape, F32),
             ),
-            in_specs=[vm] * 6 + [anyw] * 3,
+            in_specs=[anyw] * 9,
             out_specs=(anyw, anyw),
             scratch_shapes=[
+                vi(1, 1, blocks), vi(1, 1, cells), vi(1, 1, cells), vi(1, 1, cells),
+                v(1, 1, cells), vi(1, 1, cells),
                 v(6, levels, 128, 128),
                 pltpu.VMEM((6, levels * 128, 256), BF16),
-                pltpu.VMEM((n_lon, 8, 128), jnp.int32),
-                pltpu.VMEM((n_lon, 8, 128), jnp.int32),
-                v(n_lon, channels, 128),
-                v(n_lon, channels, 128),
+                vi(n_lon, 4, 128), vi(n_lon, 4, 128),
+                v(n_lon, 4 * levels, 128), v(n_lon, 4 * levels, 128),
+                v(n_lon, 2 * levels, 128), v(n_lon, 2 * levels, 128),
                 v(channels, ext, 128),
                 v(channels, ext, 128),
                 v(128, 128), v(ext, 128), v(ext, 128),
+                v(128, 128), v(128, 128), v(128, 128),
+                v(rows0, 128), v(rows0, 128), v(rows0, 128), v(rows0, 128),
+                v(rows1, 128), v(rows1, 128), v(rows1, 128), v(rows1, 128),
                 v(levels, ext, 128), v(levels, ext, 128),
                 v(128, 128), v(ext, 128), v(ext, 128),
                 v(ext, 128), v(ext, 128), v(ext, 128), v(ext, 128),
@@ -592,21 +711,21 @@
                 v(128, 128),
                 pltpu.VMEM((128, cells), BF16),
                 pltpu.VMEM((128, 2 * cells), BF16),
-                v(5, levels, 8, 128),
-                v(ndev, 8, 128),
-                v(8, 128),
+                v(5, levels, used, 128),
+                v(ndev, used, 128),
+                v(used, 128),
                 v(6, levels, 128, 128),
                 v(levels, 128, 128),
-                sem(2), sem(5), sem(3),
-                sem(n_lon), sem(n_lon), sem(n_lon), sem(n_lon),
-                sem(8), sem(8), sem(8), sem(8), sem(ndev), sem(ndev),
+                sem(8), sem(5), sem(3),
+                sem(n_lon), sem(n_lon), sem(2 * n_lon), sem(2 * n_lon),
+                sem(8), sem(8), sem(8), sem(8), sem(8), sem(8), sem(ndev), sem(ndev),
             ],
             compiler_params=pltpu.CompilerParams(
-                collective_id=0, has_side_effects=True, vmem_limit_bytes=48 * 1024 * 1024
+                collective_id=0, has_side_effects=True, vmem_limit_bytes=60 * 1024 * 1024
             ),
             name="shell_step",
         )(
-            partner, src_row, src_col, weight_id, border_angle, dest_cell,
+            partner.reshape(1, 1, blocks), src_row, src_col, weight_id, border_angle, dest_cell,
             fields, viscosity, oper,
         )
 

time: 40.3 us -> 32.7 us (0.81)
  local copies, waits for them, and re-layouts: 9.29 us -> 3.45 us
  Pallas kernels: 30 us -> 28.5 us
    unnamed x19 -> x4, local copies, waits for them, and re-layouts: 9.29 us -> 3.45 us
    pallas_call x1, Pallas kernels: 30 us -> 28.5 us  [shards(): pl.pallas_call(functools.partial(kernel, (n_lat, n_lon, levels, blocks)),...]
where the time goes in v2:
time: 32.7 us; the launch traced here: 32.6 us
  Pallas kernels  28.5 us (87%)
  local copies, waits for them, and re-layouts  3.45 us (11%)
  between operations  0.65 us (2%)
    pallas_call x1, Pallas kernels, shards(): pl.pallas_call(functools.partial(kernel, (n_lat, n_lon, levels, blocks)),...  28.5 us
    unnamed x4, local copies, waits for them, and re-layouts  3.45 us

profile of v2, /device:TPU:0, one launch (start us, length us, event | category | flops | bytes accessed | tf_op | source)
XLA Modules:
  0.0 32.6 jit_solution(12728871254150368037)
XLA Ops:
  0.6 28.5 %shell_step.1 = (f32[1,6,4,128,128]{4,3,2,1,0:T(8,128)}, f32[1,4,128,128]{3,2,1,0:T(8,128)}) custom-call(s32[1,1,8]{2,1,0:T(1,128)} %bitcast.1, s32[1,1,512]{2,1,0:T(1,128)} %row_in.1, s32[1,1,512]{2,1,0:T(1,128)} %col_in.1, s32[1,1,512]{2,1,0:T(1,128)} %wid_in.1, f32[1,1,512]{2,1,0:T(1,128)} %ang_in.1, s32[1,1,512]{2,1,0:T(1,128)} %dest_in.1, ...), custom_call_target="tpu_custom_call" | custom-call | tf_op jit(solution)/shard_map/shell_step/pallas_call | solution.py:684
  29.1 0.0 copy-start
  29.1 2.7 %copy.13 = f32[1,6,4,128,128]{4,3,2,1,0:T(8,128)} copy(f32[1,6,4,128,128]{4,3,2,1,0:T(8,128)} %get-tuple-element.4) | data formatting | bytes 3145728
  31.9 0.0 copy-done
  31.9 0.7 %copy.14 = f32[1,4,128,128]{3,2,1,0:T(8,128)} copy(f32[1,4,128,128]{3,2,1,0:T(8,128)S(1)} %copy-done) | data formatting | bytes 524288
Async XLA Ops:
  29.1 2.8 %copy-start = (f32[1,4,128,128]{3,2,1,0:T(8,128)S(1)}, f32[1,4,128,128]{3,2,1,0:T(8,128)}, u32[]{:S(2)}) copy-start(f32[1,4,128,128]{3,2,1,0:T(8,128)} %get-tuple-element.5) | copy-start | bytes 786436

commit v3 on v2

--- a/solution.py
+++ b/solution.py
@@ -81,13 +81,13 @@
 def kernel(
     dims,
     partner_in, row_in, col_in, wid_in, ang_in, dest_in, fields_ref, visc_ref, oper_ref,
-    out_ref, press_ref,
+    out_ref, press_ref, cv_ref,
     partner_ref, row_ref, col_ref, wid_ref, ang_ref, dest_ref,
     fld, fcat, ask, asked, reply0, answer0, reply1, answer1, x, hx,
     pk, pkl, pkr, pk2, pkl2, pkr2, to_up, to_dn, from_up, from_dn,
     to_up2, to_dn2, from_up2, from_dn2, va, vh, vpk, vpl, vpr,
     inv_s, gain_s, coef_a, coef_h, st, sth, p1, p1h, hit_s, rmask, cmask,
-    opr, sums, mine, onew, opress,
+    opr, sums, mine, onew, cvals,
     in_sem, op_sem, out_sem, ask_send, ask_recv, rep_send, rep_recv,
     halo_send, halo_recv, halo2_send, halo2_recv, v_send, v_recv, sum_send, sum_recv,
 ):
@@ -593,7 +593,7 @@
             lap = lap + levels_sum(x, f * levels, k, own)
             onew[f, k] = mid + va[k, own, :] * lap
     store_late = pltpu.make_async_copy(
-        onew.at[pl.ds(3, 3)], out_ref.at[0, pl.ds(3, 3)], out_sem.at[0]
+        onew.at[pl.ds(3, 3)], out_ref.at[pl.ds(3, 3)], out_sem.at[0]
     )
     store_late.start()
     for k in range(levels):
@@ -605,6 +605,13 @@
         onew[1, k] = st[levels + k, own, :] - 0.5 * diff
         onew[2, k] = st[2 * levels + k, own, :] - 0.5 * inv_o * (r - l)
 
+    store_new = pltpu.make_async_copy(
+        onew.at[pl.ds(0, 3)], out_ref.at[pl.ds(0, 3)], out_sem.at[1]
+    )
+    store_p = pltpu.make_async_copy(p1.at[:, own, :], press_ref, out_sem.at[2])
+    store_new.start()
+    store_p.start()
+
     for c in load_o:
         c.wait()
 
@@ -620,28 +627,14 @@
         return jnp.sum(jnp.sum(prod, axis=0, keepdims=True), axis=1, keepdims=True)
 
     zero = jnp.zeros((1, 1), F32)
-    mid_c = [coarse(0, k) for k in range(levels)]
-    row_o = lax.broadcasted_iota(jnp.int32, (128, 128), 0)
-    for k in range(levels):
-        up = jnp.where(a > 0, coarse(1, k), zero)
-        down = jnp.where(a < n_lat - 1, coarse(2, k), zero)
-        west = jnp.where(b > 0, coarse(3, k), zero)
-        east = jnp.where(b < n_lon - 1, coarse(4, k), zero)
-        c = mid_c[k]
-        opress[k] = p1[k, own, :] + c
-        high = mid_c[k + 1] if k + 1 < levels else zero
-        low = mid_c[k - 1] if k > 0 else zero
-        onew[0, k] = onew[0, k] - 0.5 * (high - low)
-        fix = jnp.where(row_o == 0, c - up, 0.0) + jnp.where(row_o == 127, down - c, 0.0)
-        onew[1, k] = onew[1, k] - 0.5 * fix
-        fix = jnp.where(first_o, c - west, 0.0) + jnp.where(last_o, east - c, 0.0)
-        onew[2, k] = onew[2, k] - 0.5 * inv_o * fix
-    store_new = pltpu.make_async_copy(
-        onew.at[pl.ds(0, 3)], out_ref.at[0, pl.ds(0, 3)], out_sem.at[1]
-    )
-    store_p = pltpu.make_async_copy(opress, press_ref.at[0], out_sem.at[2])
-    store_new.start()
-    store_p.start()
+    there = (None, a > 0, a < n_lat - 1, b > 0, b < n_lon - 1)
+    for t in range(5):
+        for k in range(levels):
+            c = coarse(t, k)
+            c = c if t == 0 else jnp.where(there[t], c, zero)
+            cvals[t * levels + k : t * levels + k + 1, :] = jnp.broadcast_to(c, (1, 128))
+    store_c = pltpu.make_async_copy(cvals, cv_ref, out_sem.at[3])
+    store_c.start()
 
     def end_lon(q, carry):
         ask_copy(q, b).wait_send()
@@ -662,6 +655,62 @@
     store_late.wait()
     store_new.wait()
     store_p.wait()
+    store_c.wait()
+
+
+def finish(
+    dims, part_f, part_p, cv_in, out_ref, press_ref, new, press, cvals, in_sem, out_sem
+):
+    n_lat, levels = dims
+    a = lax.axis_index("lat")
+    late, early = pl.ds(3, 3), pl.ds(0, 3)
+    loads = [
+        pltpu.make_async_copy(src, dst, in_sem.at[i])
+        for i, (src, dst) in enumerate(
+            (
+                (part_f.at[late], new.at[late]), (part_f.at[early], new.at[early]),
+                (part_p, press), (cv_in, cvals),
+            )
+        )
+    ]
+    for c in loads:
+        c.start()
+    row = lax.broadcasted_iota(jnp.int32, (128, 128), 0)
+    lane = lax.broadcasted_iota(jnp.int32, (128, 128), 1)
+    colat = math.pi / 4.0 + ((a * 128 + row).astype(F32) + 0.5) * (math.pi / 2.0) / (
+        n_lat * 128
+    )
+    inv = 1.0 / jnp.sin(colat)
+    stores = [
+        pltpu.make_async_copy(new.at[late], out_ref.at[0, late], out_sem.at[0]),
+        pltpu.make_async_copy(new.at[early], out_ref.at[0, early], out_sem.at[1]),
+        pltpu.make_async_copy(press, press_ref.at[0], out_sem.at[2]),
+    ]
+    loads[0].wait()
+    stores[0].start()
+    for c in loads[1:]:
+        c.wait()
+
+    def value(t, k):
+        at = t * levels + k
+        return cvals[at : at + 1, :]
+
+    for k in range(levels):
+        c = value(0, k)
+        press[k] = press[k] + c
+        high = value(0, k + 1) if k + 1 < levels else 0.0
+        low = value(0, k - 1) if k > 0 else 0.0
+        new[0, k] = new[0, k] - 0.5 * (high - low)
+        fix = jnp.where(row == 0, c - value(1, k), 0.0)
+        fix = jnp.where(row == 127, value(2, k) - c, fix)
+        new[1, k] = new[1, k] - 0.5 * fix
+        fix = jnp.where(lane == 0, c - value(3, k), 0.0)
+        fix = jnp.where(lane == 127, value(4, k) - c, fix)
+        new[2, k] = new[2, k] - 0.5 * inv * fix
+    stores[1].start()
+    stores[2].start()
+    for c in stores:
+        c.wait()
 
 
 def solution(mesh):
@@ -681,14 +730,15 @@
         sem = lambda n: pltpu.SemaphoreType.DMA((n,))
         rows0, rows1 = 11 * levels, 2 * levels
         used = oper.shape[2]
-        return pl.pallas_call(
+        part_f, part_p, cvals = pl.pallas_call(
             functools.partial(kernel, (n_lat, n_lon, levels, blocks)),
             out_shape=(
-                jax.ShapeDtypeStruct(fields.shape, F32),
-                jax.ShapeDtypeStruct(viscosity.shape, F32),
+                jax.ShapeDtypeStruct(fields.shape[1:], F32),
+                jax.ShapeDtypeStruct(viscosity.shape[1:], F32),
+                jax.ShapeDtypeStruct((5 * levels, 128), F32),
             ),
             in_specs=[anyw] * 9,
-            out_specs=(anyw, anyw),
+            out_specs=(anyw, anyw, anyw),
             scratch_shapes=[
                 vi(1, 1, blocks), vi(1, 1, cells), vi(1, 1, cells), vi(1, 1, cells),
                 v(1, 1, cells), vi(1, 1, cells),
@@ -715,8 +765,8 @@
                 v(ndev, used, 128),
                 v(used, 128),
                 v(6, levels, 128, 128),
-                v(levels, 128, 128),
-                sem(8), sem(5), sem(3),
+                v(5 * levels, 128),
+                sem(8), sem(5), sem(4),
                 sem(n_lon), sem(n_lon), sem(2 * n_lon), sem(2 * n_lon),
                 sem(8), sem(8), sem(8), sem(8), sem(8), sem(8), sem(ndev), sem(ndev),
             ],
@@ -728,6 +778,20 @@
             partner.reshape(1, 1, blocks), src_row, src_col, weight_id, border_angle, dest_cell,
             fields, viscosity, oper,
         )
+        return pl.pallas_call(
+            functools.partial(finish, (n_lat, levels)),
+            out_shape=(
+                jax.ShapeDtypeStruct(fields.shape, F32),
+                jax.ShapeDtypeStruct(viscosity.shape, F32),
+            ),
+            in_specs=[anyw] * 3,
+            out_specs=(anyw, anyw),
+            scratch_shapes=[
+                v(6, levels, 128, 128), v(levels, 128, 128), v(5 * levels, 128), sem(4), sem(3),
+            ],
+            compiler_params=pltpu.CompilerParams(vmem_limit_bytes=60 * 1024 * 1024),
+            name="finish",
+        )(part_f, part_p, cvals)
 
     return jax.shard_map(
         shards,

time: 32.7 us -> 31.3 us (0.957)
  local copies, waits for them, and re-layouts: 3.45 us -> 0 us
  Pallas kernels: 28.5 us -> 30.5 us
    unnamed x4 -> x0, local copies, waits for them, and re-layouts: 3.45 us -> none
    pallas_call x0 -> x1, Pallas kernels: none -> 2.5 us  [shards(): pl.pallas_call(functools.partial(finish, (n_lat, levels)), out_shape=(jax...]
    pallas_call x1, Pallas kernels: 28.5 us -> 28 us  [shards(): pl.pallas_call(functools.partial(kernel, (n_lat, n_lon, levels, blocks)),...]
where the time goes in v3:
time: 31.3 us; the launch traced here: 31.2 us
  Pallas kernels  30.5 us (97%)
  between operations  0.64 us (2%)
    pallas_call x1, Pallas kernels, shards(): pl.pallas_call(functools.partial(kernel, (n_lat, n_lon, levels, blocks)),...  28 us
    pallas_call x1, Pallas kernels, shards(): pl.pallas_call(functools.partial(finish, (n_lat, levels)), out_shape=(jax...  2.5 us

profile of v3, /device:TPU:0, one launch (start us, length us, event | category | flops | bytes accessed | tf_op | source)
XLA Modules:
  0.0 31.2 jit_solution(11435465847145108838)
XLA Ops:
  0.6 28.0 %shell_step.1 = (f32[6,4,128,128]{3,2,1,0:T(8,128)}, f32[4,128,128]{2,1,0:T(8,128)}, f32[20,128]{1,0:T(8,128)}) custom-call(s32[1,1,8]{2,1,0:T(1,128)} %bitcast.1, s32[1,1,512]{2,1,0:T(1,128)} %row_in.1, s32[1,1,512]{2,1,0:T(1,128)} %col_in.1, s32[1,1,512]{2,1,0:T(1,128)} %wid_in.1, f32[1,1,512]{2,1,0:T(1,128)} %ang_in.1, s32[1,1,512]{2,1,0:T(1,128)} %dest_in.1, ...), custom_call_target="tpu_custom_call" | custom-call | tf_op jit(solution)/shard_map/shell_step/pallas_call | solution.py:733
  28.7 2.5 %finish.1 = (f32[1,6,4,128,128]{4,3,2,1,0:T(8,128)}, f32[1,4,128,128]{3,2,1,0:T(8,128)}) custom-call(f32[6,4,128,128]{3,2,1,0:T(8,128)} %get-tuple-element.5.part_f, f32[4,128,128]{2,1,0:T(8,128)} %get-tuple-element.6.part_p, f32[20,128]{1,0:T(8,128)} %get-tuple-element.7.cv_in), custom_call_target="tpu_custom_call" | custom-call | tf_op jit(solution)/shard_map/finish/pallas_call | solution.py:781

commit v4 on v3

--- a/solution.py
+++ b/solution.py
@@ -40,7 +40,7 @@
 
 
 GROUPS = ((0, 4), (4, 6))
-WIDTHS = (3, 3, 3, 2, 1, 1)
+WIDTHS = (3, 3, 3, 3, 1, 1)
 
 
 def windows(levels, group):
@@ -53,7 +53,7 @@
 
 
 def visc_windows(levels):
-    return [(4 * k + 2, 2) for k in range(levels)]
+    return [(6 * k + 3, 3) for k in range(levels)]
 
 
 def pack(tiles, spans, lane):
@@ -70,12 +70,6 @@
     for centre, width in spans:
         mask = jnp.where((lane >= centre) & (lane < centre + width), 1, mask)
     return mask > 0
-
-
-def unpack(merged, span, lane):
-    centre, width = span
-    moved = pltpu.roll(merged, (128 - centre) % 128, 1)
-    return jnp.where((lane < width) | (lane >= 128 - width), moved, 0.0)
 
 
 def kernel(
@@ -362,7 +356,9 @@
     ca = ca - jnp.where(edge_lane, gain, 0.0)
     rim = jnp.where((row_e == TOP - 1) | (row_e == TOP + 128), 1.0, 0.0)
     coef_a[...] = jnp.where(is_own, ca, rim)
-    coef_h[...] = jnp.where(is_own & edge_lane, gain, 0.0)
+    slot6 = lane % 6
+    at_west, at_east = slot6 == 2, slot6 == 3
+    coef_h[...] = jnp.where(is_own & (at_west | at_east), gain, 0.0)
 
     replies, answers = (reply0, reply1), (answer0, answer1)
 
@@ -416,8 +412,13 @@
     lax.fori_loop(0, n_lon // 2, functools.partial(serve, 1), 0)
     halo_wait_recv(vargs)
     vmerged = jnp.where(right_part(visc_windows(levels), lane), vpr[...], vpl[...])
-    for k in range(levels):
-        vh[k] = unpack(vmerged, visc_windows(levels)[k], lane)
+    span_f = 6 * levels
+    vh[...] = jnp.where(
+        lane < span_f, vmerged,
+        jnp.where(
+            lane < 2 * span_f, pltpu.roll(vmerged, span_f, 1), pltpu.roll(vmerged, 2 * span_f, 1)
+        ),
+    )
 
     half_row = half[0:1]
 
@@ -480,21 +481,40 @@
     unpack_rows(GROUPS[0], hargs[0])
     spans = windows(levels, GROUPS[0])
     merged = jnp.where(right_part(spans, lane), pkr[...], pkl[...])
-    for c, span in enumerate(spans):
-        hx[c] = unpack(merged, span, lane)
+    hx[...] = merged
+    own_edges = jnp.concatenate(
+        [
+            pack([x[c, 0:TOP, :] for c in range(4 * levels)], spans, lane8),
+            pk[...],
+            pack([x[c, TOP + 128 : rows_ext, :] for c in range(4 * levels)], spans, lane8),
+        ],
+        axis=0,
+    )
 
     rows_ok = ((row_e >= TOP) | (a > 0)) & ((row_e < TOP + 128) | (a < n_lat - 1))
-    lanes_ok = ((lane >= 64) | (b < n_lon - 1)) & ((lane < 64) | (b > 0))
+    lanes_ok = ((slot6 >= 3) | (b > 0)) & ((slot6 < 3) | (b < n_lon - 1))
     halo_ok = rows_ok & lanes_ok
+    level = (lane // 6) % levels
     first, last = lane == 0, lane == 127
 
-    def sides(body, rim):
-        ra, rh = pltpu.roll(body, 127, 1), pltpu.roll(rim, 127, 1)
-        la, lh = pltpu.roll(body, 1, 1), pltpu.roll(rim, 1, 1)
-        return (
-            jnp.where(last, rh, ra), jnp.where(first, lh, la),
-            jnp.where(last, ra, rh), jnp.where(first, la, lh),
-        )
+    def sides(body, strip, centre, at_first, at_last):
+        r = jnp.where(
+            at_last, pltpu.roll(strip, (127 - centre) % 128, 1), pltpu.roll(body, 127, 1)
+        )
+        l = jnp.where(
+            at_first, pltpu.roll(strip, (129 - centre) % 128, 1), pltpu.roll(body, 1, 1)
+        )
+        return r, l
+
+    def strip_sides(strip, edges):
+        r = jnp.where(at_west, pltpu.roll(edges, 127, 1), pltpu.roll(strip, 127, 1))
+        l = jnp.where(at_east, pltpu.roll(edges, 1, 1), pltpu.roll(strip, 1, 1))
+        return r, l
+
+    def strip_levels(strip):
+        up = jnp.where(level < levels - 1, pltpu.roll(strip, 122, 1), 0.0)
+        down = jnp.where(level > 0, pltpu.roll(strip, 6, 1), 0.0)
+        return up, down
 
     def next_row(v):
         return pltpu.roll(v, rows_ext - 1, 0)
@@ -516,39 +536,47 @@
         return up - down
 
     gain = gain_s[...]
+    mid = 4.0 + 2.0 * gain
     for f in range(3):
         for k in range(levels):
             c = f * levels + k
-            body, rim = x[c], hx[c]
-            r, l, rr, ll = sides(body, rim)
-            mid = 4.0 + 2.0 * gain
+            body = x[c]
+            r, l = sides(body, hx[...], spans[c][0], first, last)
             lap = next_row(body) + prev_row(body) + gain * (r + l) - mid * body
             lap = lap + levels_sum(x, f * levels, k)
             new = body + va[k] * lap
-            lap_h = next_row(rim) + prev_row(rim) + gain * (rr + ll) - mid * rim
-            lap_h = lap_h + levels_sum(hx, f * levels, k)
-            new_h = rim + vh[k] * lap_h
             if f == 0:
                 new = new + BUOYANCY * x[3 * levels + k]
-                new_h = new_h + BUOYANCY * hx[3 * levels + k]
             st[c] = jnp.where(rows_ok, new, 0.0)
-            sth[c] = jnp.where(halo_ok, new_h, 0.0)
-
-    scale = -0.5 / (4.0 + 2.0 * gain)
+    strip = hx[...]
+    r, l = strip_sides(strip, own_edges)
+    up, down = strip_levels(strip)
+    lap = next_row(strip) + prev_row(strip) + gain * (r + l) - mid * strip + (up + down)
+    new = strip + vh[...] * lap
+    warm = pltpu.roll(strip, 128 - 3 * span_f, 1)
+    new = new + jnp.where(lane < span_f, BUOYANCY * warm, 0.0)
+    sth[...] = jnp.where(halo_ok & (lane < 3 * span_f), new, 0.0)
+
+    scale = -0.5 / mid
     for k in range(levels):
-        r, l, rr, ll = sides(st[2 * levels + k], sth[2 * levels + k])
-        b1, h1 = st[levels + k], sth[levels + k]
+        r, l = sides(st[2 * levels + k], sth[...], spans[2 * levels + k][0], first, last)
+        b1 = st[levels + k]
         d = next_row(b1) - prev_row(b1) + inv_s[...] * (r - l) + levels_diff(st, 0, k)
-        dh = next_row(h1) - prev_row(h1) + inv_s[...] * (rr - ll) + levels_diff(sth, 0, k)
         p1[k] = jnp.where(rows_ok, scale * d, 0.0)
-        p1h[k] = jnp.where(halo_ok, scale * dh, 0.0)
+    strip = sth[...]
+    edges = pack([st[2 * levels + k] for k in range(levels)], spans[0:levels], lane)
+    r, l = strip_sides(pltpu.roll(strip, 128 - 2 * span_f, 1), edges)
+    one = pltpu.roll(strip, 128 - span_f, 1)
+    up, down = strip_levels(strip)
+    d = next_row(one) - prev_row(one) + inv_s[...] * (r - l) + (up - down)
+    p1h[...] = jnp.where(halo_ok & (lane < span_f), scale * d, 0.0)
 
     shape = mine.shape
     place = lax.broadcasted_iota(jnp.int32, shape, 0) * 128
     place = place + lax.broadcasted_iota(jnp.int32, shape, 1)
     tile = jnp.zeros(shape, F32)
     for k in range(levels):
-        part = coef_a[...] * p1[k] + coef_h[...] * p1h[k]
+        part = coef_a[...] * p1[k] + jnp.where(lane // 6 == k, coef_h[...] * p1h[...], 0.0)
         part = part + jnp.where(is_own, levels_sum(p1, 0, k), 0.0)
         total = jnp.sum(jnp.sum(part, axis=0, keepdims=True), axis=1, keepdims=True)
         tile = tile + jnp.where(place == me * levels + k, total * (1.0 / 128.0), 0.0)
@@ -571,23 +599,19 @@
     inv_o = inv_s[own, :]
     first_o, last_o = lane_o == 0, lane_o == 127
 
-    def sides_own(body, rim):
-        r = jnp.where(last_o, pltpu.roll(rim, 127, 1), pltpu.roll(body, 127, 1))
-        l = jnp.where(first_o, pltpu.roll(rim, 1, 1), pltpu.roll(body, 1, 1))
-        return r, l
-
     halo_wait_recv(hargs[1])
     unpack_rows(GROUPS[1], hargs[1])
-    spans = windows(levels, GROUPS[1])
-    merged = jnp.where(right_part(spans, lane_o), pkr2[...], pkl2[...])
-    for c, span in enumerate(spans):
-        hx[4 * levels + c, own, :] = unpack(merged, span, lane_o)
+    spans2 = windows(levels, GROUPS[1])
+    merged2 = jnp.where(right_part(spans2, lane_o), pkr2[...], pkl2[...])
     for f in range(3, 6):
         for k in range(levels):
             c = f * levels + k
             body = x[c]
             mid = body[TOP : TOP + 128]
-            r, l = sides_own(mid, hx[c, own, :])
+            if f == 3:
+                r, l = sides(mid, hx[own, :], spans[c][0], first_o, last_o)
+            else:
+                r, l = sides(mid, merged2, spans2[c - 4 * levels][0], first_o, last_o)
             lap = next_row(body)[TOP : TOP + 128] + prev_row(body)[TOP : TOP + 128]
             lap = lap + gain_o * (r + l) - (4.0 + 2.0 * gain_o) * mid
             lap = lap + levels_sum(x, f * levels, k, own)
@@ -599,7 +623,7 @@
     for k in range(levels):
         body = p1[k]
         mid = body[TOP : TOP + 128]
-        r, l = sides_own(mid, p1h[k, own, :])
+        r, l = sides(mid, p1h[own, :], spans[k][0], first_o, last_o)
         diff = next_row(body)[TOP : TOP + 128] - prev_row(body)[TOP : TOP + 128]
         onew[0, k] = st[k, own, :] - 0.5 * levels_diff(p1, 0, k, own)
         onew[1, k] = st[levels + k, own, :] - 0.5 * diff
@@ -728,7 +752,7 @@
         v = lambda *s: pltpu.VMEM(s, F32)
         vi = lambda *s: pltpu.VMEM(s, jnp.int32)
         sem = lambda n: pltpu.SemaphoreType.DMA((n,))
-        rows0, rows1 = 11 * levels, 2 * levels
+        rows0, rows1 = 12 * levels, 2 * levels
         used = oper.shape[2]
         part_f, part_p, cvals = pl.pallas_call(
             functools.partial(kernel, (n_lat, n_lon, levels, blocks)),
@@ -748,16 +772,16 @@
                 v(n_lon, 4 * levels, 128), v(n_lon, 4 * levels, 128),
                 v(n_lon, 2 * levels, 128), v(n_lon, 2 * levels, 128),
                 v(channels, ext, 128),
-                v(channels, ext, 128),
+                v(ext, 128),
                 v(128, 128), v(ext, 128), v(ext, 128),
                 v(128, 128), v(128, 128), v(128, 128),
                 v(rows0, 128), v(rows0, 128), v(rows0, 128), v(rows0, 128),
                 v(rows1, 128), v(rows1, 128), v(rows1, 128), v(rows1, 128),
-                v(levels, ext, 128), v(levels, ext, 128),
+                v(levels, ext, 128), v(ext, 128),
                 v(128, 128), v(ext, 128), v(ext, 128),
                 v(ext, 128), v(ext, 128), v(ext, 128), v(ext, 128),
-                v(3 * levels, ext, 128), v(3 * levels, ext, 128),
-                v(levels, ext, 128), v(levels, ext, 128),
+                v(3 * levels, ext, 128), v(ext, 128),
+                v(levels, ext, 128), v(ext, 128),
                 v(128, 128),
                 pltpu.VMEM((128, cells), BF16),
                 pltpu.VMEM((128, 2 * cells), BF16),

time: 31.3 us -> 31.2 us (level)
  no operation moved by 1% of the time
where the time goes in v4:
time: 31.2 us; the launch traced here: 31 us
  Pallas kernels  30.4 us (97%)
  between operations  0.64 us (2%)
    pallas_call x1, Pallas kernels, shards(): pl.pallas_call(functools.partial(kernel, (n_lat, n_lon, levels, blocks)),...  27.9 us
    pallas_call x1, Pallas kernels, shards(): pl.pallas_call(functools.partial(finish, (n_lat, levels)), out_shape=(jax...  2.5 us

profile of v4, /device:TPU:0, one launch (start us, length us, event | category | flops | bytes accessed | tf_op | source)
XLA Modules:
  0.0 31.0 jit_solution(5264974476806410353)
XLA Ops:
  0.6 27.9 %shell_step.1 = (f32[6,4,128,128]{3,2,1,0:T(8,128)}, f32[4,128,128]{2,1,0:T(8,128)}, f32[20,128]{1,0:T(8,128)}) custom-call(s32[1,1,8]{2,1,0:T(1,128)} %bitcast.1, s32[1,1,512]{2,1,0:T(1,128)} %row_in.1, s32[1,1,512]{2,1,0:T(1,128)} %col_in.1, s32[1,1,512]{2,1,0:T(1,128)} %wid_in.1, f32[1,1,512]{2,1,0:T(1,128)} %ang_in.1, s32[1,1,512]{2,1,0:T(1,128)} %dest_in.1, ...), custom_call_target="tpu_custom_call" | custom-call | tf_op jit(solution)/shard_map/shell_step/pallas_call | solution.py:757
  28.5 2.5 %finish.1 = (f32[1,6,4,128,128]{4,3,2,1,0:T(8,128)}, f32[1,4,128,128]{3,2,1,0:T(8,128)}) custom-call(f32[6,4,128,128]{3,2,1,0:T(8,128)} %get-tuple-element.5.part_f, f32[4,128,128]{2,1,0:T(8,128)} %get-tuple-element.6.part_p, f32[20,128]{1,0:T(8,128)} %get-tuple-element.7.cv_in), custom_call_target="tpu_custom_call" | custom-call | tf_op jit(solution)/shard_map/finish/pallas_call | solution.py:805

commit v5 on v4

--- a/solution.py
+++ b/solution.py
@@ -37,6 +37,10 @@
     wide = np.zeros((count, used * 128), np.float32)
     wide[:, :count] = full
     return wide.reshape(n_lat * n_lon, levels, used, 128)
+
+
+def short_loop(start, end, body, init):
+    return lax.fori_loop(start, end, body, init, unroll=end - start <= 16)
 
 
 GROUPS = ((0, 4), (4, 6))
@@ -138,13 +142,13 @@
         )
         return carry
 
-    lax.fori_loop(1, ndev, greet, 0)
+    short_loop(1, ndev, greet, 0)
 
     def greet_other(i, carry):
         pl.semaphore_signal(barrier, inc=1, device_id=dev(1 - p, a, i), device_id_type=MESH)
         return carry
 
-    lax.fori_loop(0, n_lon, greet_other, 0)
+    short_loop(0, n_lon, greet_other, 0)
 
     lane8 = lax.broadcasted_iota(jnp.int32, (8, 128), 1)
     sub8 = lax.broadcasted_iota(jnp.int32, (8, 128), 0)
@@ -201,7 +205,7 @@
         ask_copy(q, b).start()
         return carry
 
-    lax.fori_loop(0, n_lon, send_ask, 0)
+    short_loop(0, n_lon, send_ask, 0)
 
     ways = [(da, db) for da in (-1, 0, 1) for db in (-1, 0, 1) if (da, db) != (0, 0)]
 
@@ -429,7 +433,7 @@
             rep_copy(g, 0, q).wait_recv()
             return carry
 
-        lax.fori_loop(0, n_lon, wait_rep, 0)
+        short_loop(0, n_lon, wait_rep, 0)
         got = [answers[g][q] for q in range(n_lon)]
         got_r = [pltpu.roll(v, 64, 1) for v in got]
         picked = []
@@ -593,7 +597,7 @@
         sum_copy(lax.rem(me + i, ndev), me, i).start()
         return carry
 
-    lax.fori_loop(1, ndev, send_sum, 0)
+    short_loop(1, ndev, send_sum, 0)
 
     gain_o = gain_s[own, :]
     inv_o = inv_s[own, :]
@@ -644,7 +648,7 @@
         sum_copy(me, s, 0).wait_recv()
         return total + sums[s]
 
-    vec = lax.fori_loop(1, ndev, take_sum, mine[...])
+    vec = short_loop(1, ndev, take_sum, mine[...])
 
     def coarse(t, k):
         prod = opr[t, k] * vec
@@ -666,7 +670,7 @@
         rep_copy(1, q, b).wait_send()
         return carry
 
-    lax.fori_loop(0, n_lon, end_lon, 0)
+    short_loop(0, n_lon, end_lon, 0)
     halo_wait_send(vargs)
     halo_wait_send(hargs[0])
     halo_wait_send(hargs[1])
@@ -675,7 +679,7 @@
         sum_copy(me, me, i).wait_send()
         return carry
 
-    lax.fori_loop(1, ndev, end_sum, 0)
+    short_loop(1, ndev, end_sum, 0)
     store_late.wait()
     store_new.wait()
     store_p.wait()

time: 31.2 us -> 31.1 us (level)
  no operation moved by 1% of the time
where the time goes in v5:
time: 31.1 us; the launch traced here: 30.9 us
  Pallas kernels  30.3 us (97%)
  between operations  0.64 us (2%)
    pallas_call x1, Pallas kernels, shards(): pl.pallas_call(functools.partial(kernel, (n_lat, n_lon, levels, blocks)),...  27.8 us
    pallas_call x1, Pallas kernels, shards(): pl.pallas_call(functools.partial(finish, (n_lat, levels)), out_shape=(jax...  2.5 us

profile of v5, /device:TPU:0, one launch (start us, length us, event | category | flops | bytes accessed | tf_op | source)
XLA Modules:
  0.0 30.9 jit_solution(5037363594400107415)
XLA Ops:
  0.6 27.8 %shell_step.1 = (f32[6,4,128,128]{3,2,1,0:T(8,128)}, f32[4,128,128]{2,1,0:T(8,128)}, f32[20,128]{1,0:T(8,128)}) custom-call(s32[1,1,8]{2,1,0:T(1,128)} %bitcast.1, s32[1,1,512]{2,1,0:T(1,128)} %row_in.1, s32[1,1,512]{2,1,0:T(1,128)} %col_in.1, s32[1,1,512]{2,1,0:T(1,128)} %wid_in.1, f32[1,1,512]{2,1,0:T(1,128)} %ang_in.1, s32[1,1,512]{2,1,0:T(1,128)} %dest_in.1, ...), custom_call_target="tpu_custom_call" | custom-call | tf_op jit(solution)/shard_map/shell_step/pallas_call | solution.py:761
  28.4 2.5 %finish.1 = (f32[1,6,4,128,128]{4,3,2,1,0:T(8,128)}, f32[1,4,128,128]{3,2,1,0:T(8,128)}) custom-call(f32[6,4,128,128]{3,2,1,0:T(8,128)} %get-tuple-element.5.part_f, f32[4,128,128]{2,1,0:T(8,128)} %get-tuple-element.6.part_p, f32[20,128]{1,0:T(8,128)} %get-tuple-element.7.cv_in), custom_call_target="tpu_custom_call" | custom-call | tf_op jit(solution)/shard_map/finish/pallas_call | solution.py:809
